TPU v7x, 32 devices: a whole 2x2x4 slice. The times are simulated.
32 devices in a mesh: grp: 1, dap: 32 (over z, y, x, core), ch: 1.
Axes of the slice: x: 2, y: 2, z: 4, core: 2. Of those that a mesh axis runs over, the one named last changes fastest.
Arguments:
- pair_act: bfloat16 [128, 128, 128], P(('grp', 'dap')), may hold values from -24 to 24
- out_grad: bfloat16 [128, 128, 128], P(('grp', 'dap'), 'ch'), may hold values from -6 to 6
- residue_mask: int32 [128], P('grp'), may hold values 0 or 1
- ln_in_gain: float32 [128], replicated, may hold values from 0.1 to 1.9
- ln_in_bias: float32 [128], replicated, may hold values from -3 to 3
- w_a_proj: bfloat16 [128, 128], P(None, 'ch'), may hold values from -4 to 4
- w_a_gate: bfloat16 [128, 128], P(None, 'ch'), may hold values from -0.5 to 0.5
- w_b_proj: bfloat16 [128, 128], P(None, 'ch'), may hold values from -0.5 to 0.5
- w_b_gate: bfloat16 [128, 128], P(None, 'ch'), may hold values from -0.5 to 0.5
- w_gate: bfloat16 [128, 128], replicated, may hold values from -0.5 to 0.5
- ln_out_gain: float32 [128], replicated, may hold values from 0.1 to 1.9
- ln_out_bias: float32 [128], replicated, may hold values from -4 to 4
- w_out: bfloat16 [128, 128], replicated, may hold values from -0.5 to 0.5
Outputs:
- pair_grad: bfloat16 [128, 128, 128], P(('grp', 'dap'), 'ch')
All inputs are finite; a program needn't handle non-finite values.
Results may differ from a plain program's by a relative error of at most 0.009.
Values may be sent and summed in bfloat16 or wider, within the bound.
No kernel may reach another device: no remote copies, remote signals or barrier semaphores. Data moves between devices by JAX's collectives and lax.ppermute only.
A program may use at most 128 MiB of HBM per device.

v0:
```python
import jax
import jax.numpy as jnp
from jax import lax
from jax.sharding import PartitionSpec as P

EPSILON = 1e-05


def normalise(values, reduce_dim):
    centre = values - jnp.mean(values, axis=reduce_dim, keepdims=True)
    inverse = lax.rsqrt(jnp.mean(centre * centre, axis=reduce_dim, keepdims=True) + EPSILON)
    return (centre * inverse, inverse)


def norm_backward(grad_hat, normed, inverse, reduce_dim):
    mean_grad = jnp.mean(grad_hat, axis=reduce_dim, keepdims=True)
    mean_proj = jnp.mean(grad_hat * normed, axis=reduce_dim, keepdims=True)
    return inverse * (grad_hat - mean_grad - normed * mean_proj)


def on_device(
    pair_act,
    out_grad,
    residue_mask,
    ln_in_gain,
    ln_in_bias,
    w_a_proj,
    w_a_gate,
    w_b_proj,
    w_b_gate,
    w_gate,
    ln_out_gain,
    ln_out_bias,
    w_out,
):
    own_rows = pair_act.shape[0]
    col_span = out_grad.shape[1]
    hidden_local = w_a_proj.shape[1]
    row_first = lax.axis_index("dap") * own_rows
    col_first = lax.axis_index("ch") * col_span
    normed_in, rstd_in = normalise(pair_act.astype(jnp.float32), 2)
    pair_norm = (normed_in * ln_in_gain + ln_in_bias).astype(jnp.bfloat16)
    valid_all = residue_mask.astype(jnp.float32)
    valid_rows = lax.dynamic_slice_in_dim(valid_all, row_first, own_rows)
    row_mask = (valid_rows[:, None] * valid_all[None, :])[None]
    w_four = jnp.concatenate((w_a_proj, w_a_gate, w_b_proj, w_b_gate), axis=1)
    projected = jnp.einsum("ikc,cg->gik", pair_norm, w_four, preferred_element_type=jnp.float32)
    a_proj = projected[:hidden_local]
    a_sig = jax.nn.sigmoid(projected[hidden_local : 2 * hidden_local])
    b_proj = projected[2 * hidden_local : 3 * hidden_local]
    b_sig = jax.nn.sigmoid(projected[3 * hidden_local :])
    edge_a = (row_mask * a_sig * a_proj).astype(jnp.bfloat16)
    edge_b = (row_mask * b_sig * b_proj).astype(jnp.bfloat16)
    edge_b_all = lax.all_gather(edge_b, "dap", axis=1, tiled=True)
    tri_sum = jnp.einsum(
        "hik,hjk->hij", edge_a, edge_b_all, preferred_element_type=jnp.float32
    ).astype(jnp.bfloat16)
    tri_full = lax.all_to_all(tri_sum, "ch", split_axis=2, concat_axis=0, tiled=True)
    normed_out, rstd_out = normalise(tri_full.astype(jnp.float32), 0)
    gain_out = ln_out_gain.reshape(-1, 1, 1)
    bias_out = ln_out_bias.reshape(-1, 1, 1)
    tri_norm = (normed_out * gain_out + bias_out).astype(jnp.bfloat16)
    proj_out = jnp.einsum("hij,hc->ijc", tri_norm, w_out, preferred_element_type=jnp.float32)
    norm_cols = lax.dynamic_slice_in_dim(pair_norm, col_first, col_span, 1)
    gate_act = jax.nn.sigmoid(
        jnp.einsum("ijc,cd->ijd", norm_cols, w_gate, preferred_element_type=jnp.float32)
    )
    upstream = out_grad.astype(jnp.float32)
    d_proj = (upstream * gate_act).astype(jnp.bfloat16)
    d_gate = (upstream * proj_out * gate_act * (1.0 - gate_act)).astype(jnp.bfloat16)
    d_normed = (
        jnp.einsum("ijc,hc->hij", d_proj, w_out, preferred_element_type=jnp.float32) * gain_out
    )
    d_tri = norm_backward(d_normed, normed_out, rstd_out, 0).astype(jnp.bfloat16)
    d_split = lax.all_to_all(d_tri, "ch", split_axis=0, concat_axis=2, tiled=True)
    d_edge_a = jnp.einsum("hij,hjk->hik", d_split, edge_b_all, preferred_element_type=jnp.float32)
    d_edge_b = jnp.transpose(
        lax.psum_scatter(
            jnp.einsum("hij,hik->jhk", d_split, edge_a, preferred_element_type=jnp.float32),
            "dap",
            scatter_dimension=0,
            tiled=True,
        ),
        (1, 0, 2),
    )

    def split_grad(d_edge, sig_val, proj_val):
        masked = d_edge * row_mask
        return (
            (masked * sig_val).astype(jnp.bfloat16),
            (masked * proj_val * sig_val * (1.0 - sig_val)).astype(jnp.bfloat16),
        )

    d_four = jnp.concatenate(
        split_grad(d_edge_a, a_sig, a_proj) + split_grad(d_edge_b, b_sig, b_proj), axis=0
    )
    d_hidden = jnp.einsum("gik,cg->ikc", d_four, w_four, preferred_element_type=jnp.float32)
    d_share = lax.psum_scatter(
        d_hidden.astype(jnp.bfloat16), "ch", scatter_dimension=1, tiled=True
    ).astype(jnp.float32)
    d_pair_norm = d_share + jnp.einsum(
        "ijd,cd->ijc", d_gate, w_gate, preferred_element_type=jnp.float32
    )
    normed_cols = lax.dynamic_slice_in_dim(normed_in, col_first, col_span, 1)
    rstd_cols = lax.dynamic_slice_in_dim(rstd_in, col_first, col_span, 1)
    grad_hat = d_pair_norm * ln_in_gain
    return norm_backward(grad_hat, normed_cols, rstd_cols, 2).astype(jnp.bfloat16)


def solution(mesh):
    in_specs = (
        P(("grp", "dap"), None, None),
        P(("grp", "dap"), "ch", None),
        P("grp"),
        P(),
        P(),
        P(None, "ch"),
        P(None, "ch"),
        P(None, "ch"),
        P(None, "ch"),
        P(),
        P(),
        P(),
        P(),
    )
    out_specs = P(("grp", "dap"), "ch", None)
    return jax.shard_map(
        on_device, mesh=mesh, in_specs=in_specs, out_specs=out_specs, check_vma=False
    )
```

profile of v0, /device:TPU:0, one launch (start us, length us, event | category | flops | bytes accessed | tf_op | source)
XLA Modules:
  0.0 257.0 jit_solution(17985433581288274531)
XLA Ops:
  6.5 0.0 copy-start
  6.5 0.0 all-gather.2.cloned.1.call-start
  6.5 0.7 convert_element_type.58
  7.2 0.1 dynamic_slice.2
  7.3 0.1 broadcast_multiply_fusion
  7.4 0.9 copy.47
  8.2 0.9 copy.48
  9.1 0.9 copy.49
  10.0 0.9 copy.50
  10.9 1.0 copy.46
  11.9 0.1 fusion.44
  12.0 1.0 fusion.72
  13.0 0.0 copy-start.1
  13.1 0.0 copy-start.4
  13.1 0.8 multiply_convert_fusion.3
  13.9 0.0 all-gather.2.cloned.1.call-update
  13.9 0.0 reduce-scatter.2.cloned.1.call-start
  13.9 1.1 fusion.10
  15.1 63.7 %all-gather.2.cloned.1.call-done = bf16[128,128,128]{2,0,1:T(8,128)(2,1)} async-done(((bf16[128,4,128]{2,0,1:T(8,128)(2,1)}), bf16[128,128,128]{2,0,1:T(8,128)(2,1)}) %all-gather.2.cloned.1.call-update) | async-done | bytes 4194320 | tf_op jit(solution)/shard_map/all_gather | solution.py:54
  78.8 5.8 %fusion.2 = bf16[128,4,128]{2,1,0:T(4,128)(2,1)S(1)} fusion(bf16[128,128,128]{2,0,1:T(8,128)(2,1)} %all-gather.2.cloned.1.call-done, bf16[128,4,128]{2,0,1:T(8,128)(2,1)S(1)} %get-tuple-element.15), kind=kOutput, calls=%fused_computation.2 | convolution fusion | flops 16777216 | bytes 4456448 | tf_op jit(solution)/shard_map/hik,hjk->hij/dot_general | solution.py:55
  84.6 0.1 copy.54
  84.7 0.1 convert_reduce_fusion
  84.9 0.2 fusion.37
  85.1 0.0 copy-done
  85.1 0.0 copy-done.1
  85.1 0.0 copy-done.4
  85.1 0.4 fusion.84
  85.6 0.3 fusion.34
  85.9 0.1 copy.57
  86.1 4.5 %fusion.69 = f32[128,128,128]{2,1,0:T(8,128)} fusion(bf16[128,4,128]{2,1,0:T(4,128)(2,1)S(1)} %copy.57, bf16[128,4,128]{2,0,1:T(8,128)(2,1)S(1)} %get-tuple-element.15), kind=kOutput, calls=%fused_computation.82 | convolution fusion | flops 16777216 | bytes 8650752 | tf_op jit(solution)/shard_map/hij,hik->jhk/dot_general | solution.py:79
  90.6 9.3 %copy.62 = f32[128,128,128]{1,0,2:T(8,128)} copy(f32[128,128,128]{2,1,0:T(8,128)} %fusion.69) | data formatting | bytes 16777216 | tf_op jit(solution)/shard_map/hij,hik->jhk/dot_general | solution.py:79
  99.9 0.0 reduce-scatter.2.cloned.1.call-update
  99.9 0.0 copy-start.2
  99.9 0.0 copy-start.3
  99.9 0.0 copy-start.5
  99.9 5.7 %fusion = f32[128,4,128]{2,1,0:T(4,128)S(1)} fusion(bf16[128,4,128]{2,1,0:T(4,128)(2,1)S(1)} %copy.57, bf16[128,128,128]{2,0,1:T(8,128)(2,1)} %all-gather.2.cloned.1.call-done), kind=kOutput, calls=%fused_computation | convolution fusion | flops 16777216 | bytes 4587520 | tf_op jit(solution)/shard_map/hij,hjk->hik/dot_general | solution.py:76
  105.7 141.6 %reduce-scatter.2.cloned.1.call-done = f32[4,128,128]{2,1,0:T(8,128)} async-done(((f32[128,128,128]{2,1,0:T(8,128)}), f32[4,128,128]{2,1,0:T(8,128)}) %reduce-scatter.2.cloned.1.call-update) | async-done | bytes 262160 | tf_op jit(solution)/shard_map/reduce_scatter | solution.py:78
  247.2 1.2 multiply_convert_fusion.1
  248.4 0.3 fusion.12
  248.7 0.0 copy-done.2
  248.7 0.0 copy-done.3
  248.7 0.0 copy-done.5
  248.7 0.5 fusion.83
  249.3 0.1 fusion.43
  249.3 0.8 copy.64
  (8 shorter events, 0.1 us)
Async XLA Ops:
  6.5 78.6 %copy-start = (bf16[128,128]{1,0:T(8,128)(2,1)S(1)}, bf16[128,128]{1,0:T(8,128)(2,1)}, u32[]{:S(2)}) copy-start(bf16[128,128]{1,0:T(8,128)(2,1)} %param.25) | copy-start | bytes 98308
  6.5 72.3 %all-gather.2.cloned.1.call-start = ((), (), s32[]{:S(2)}) async-start(), calls=%async_computation.1 | async-start | bytes 4325376 | tf_op jit(solution)/shard_map/all_gather | solution.py:54
  13.0 72.1 %copy-start.1 = (bf16[4,128,128]{2,1,0:T(8,128)(2,1)S(1)}, bf16[4,128,128]{2,1,0:T(8,128)(2,1)}, u32[]{:S(2)}) copy-start(bf16[4,128,128]{2,1,0:T(8,128)(2,1)} %param.14) | copy-start | bytes 393220
  13.1 72.1 %copy-start.4 = (f32[128]{0:T(128)S(1)}, f32[128]{0:T(128)}, u32[]{:S(2)}) copy-start(f32[128]{0:T(128)} %param.23) | copy-start | bytes 1540
  13.9 233.3 %reduce-scatter.2.cloned.1.call-start = ((), (), s32[]{:S(2)}) async-start(), calls=%async_computation.2 | async-start | bytes 8650752 | tf_op jit(solution)/shard_map/reduce_scatter | solution.py:78
  99.9 148.8 %copy-start.2 = (bf16[128,128]{1,0:T(8,128)(2,1)S(1)}, bf16[128,128]{1,0:T(8,128)(2,1)}, u32[]{:S(2)}) copy-start(bf16[128,128]{1,0:T(8,128)(2,1)} %param.22) | copy-start | bytes 98308
  99.9 148.8 %copy-start.3 = (f32[128]{0:T(128)S(1)}, f32[128]{0:T(128)}, u32[]{:S(2)}) copy-start(f32[128]{0:T(128)} %param.16) | copy-start | bytes 1540
  99.9 148.8 %copy-start.5 = (f32[128]{0:T(128)S(1)}, f32[128]{0:T(128)}, u32[]{:S(2)}) copy-start(f32[128]{0:T(128)} %param.24) | copy-start | bytes 1540
Sparse Core Ops, SparseCore 0:
  14.0 64.7 all-gather.1
  100.0 147.1 reduce-scatter.1
where the time goes:
time: 258 us; the launch traced here: 257 us
  waiting for transfers between devices  205 us (79%)
  matrix products  19.4 us (8%)
  local copies, waits for them, and re-layouts  15 us (6%)
  between operations  13.6 us (5%)
  other arithmetic  3.63 us (1%)
    reduce_scatter x1, waiting for transfers between devices, on_device(): lax.psum_scatter(jnp.einsum('hij,hik->jhk', d_split, edge_a, preferred_el...  142 us
    all_gather x1, waiting for transfers between devices, on_device(): edge_b_all = lax.all_gather(edge_b, 'dap', axis=1, tiled=True)  63.7 us
    dot_general x1, local copies, waits for them, and re-layouts, on_device(): jnp.einsum('hij,hik->jhk', d_split, edge_a, preferred_element_type=jnp.fl...  9.3 us
    dot_general x1, matrix products, on_device(): jnp.einsum('hik,hjk->hij', edge_a, edge_b_all, preferred_element_type=jnp...  5.79 us
    dot_general x1, matrix products, on_device(): jnp.einsum('hij,hjk->hik', d_split, edge_b_all, preferred_element_type=jn...  5.73 us
  transfers between devices with their start and end apart: 2, of which 2 were waited for; matrix products, arithmetic and copies ran while one was open for 3% of the time, Pallas kernels for 0%

commit v1 on v0

--- a/solution.py
+++ b/solution.py
@@ -19,6 +19,8 @@
 
 
 def on_device(
+    dap,
+    ch,
     pair_act,
     out_grad,
     residue_mask,
@@ -33,9 +35,10 @@
     ln_out_bias,
     w_out,
 ):
-    own_rows = pair_act.shape[0]
+    own_rows, all_cols = pair_act.shape[:2]
     col_span = out_grad.shape[1]
     hidden_local = w_a_proj.shape[1]
+    slice_h = hidden_local // dap
     row_first = lax.axis_index("dap") * own_rows
     col_first = lax.axis_index("ch") * col_span
     normed_in, rstd_in = normalise(pair_act.astype(jnp.float32), 2)
@@ -51,11 +54,21 @@
     b_sig = jax.nn.sigmoid(projected[3 * hidden_local :])
     edge_a = (row_mask * a_sig * a_proj).astype(jnp.bfloat16)
     edge_b = (row_mask * b_sig * b_proj).astype(jnp.bfloat16)
-    edge_b_all = lax.all_gather(edge_b, "dap", axis=1, tiled=True)
-    tri_sum = jnp.einsum(
-        "hik,hjk->hij", edge_a, edge_b_all, preferred_element_type=jnp.float32
-    ).astype(jnp.bfloat16)
-    tri_full = lax.all_to_all(tri_sum, "ch", split_axis=2, concat_axis=0, tiled=True)
+
+    split = (dap, slice_h, own_rows, all_cols)
+    edges = jnp.stack((edge_a.reshape(split), edge_b.reshape(split)), axis=1)
+    edges = lax.all_to_all(edges, "dap", split_axis=0, concat_axis=0, tiled=True)
+    edges = jnp.transpose(edges, (1, 2, 0, 3, 4)).reshape(2, slice_h, dap * own_rows, all_cols)
+    a_all, b_all = edges[0], edges[1]
+    tri = jnp.einsum("hik,hjk->hij", a_all, b_all, preferred_element_type=jnp.float32).astype(
+        jnp.bfloat16
+    )
+    tri = tri.reshape(slice_h, dap, own_rows, ch, col_span)
+    tri = jnp.transpose(tri, (1, 3, 0, 2, 4)).reshape(dap * ch, slice_h, own_rows, col_span)
+    tri = lax.all_to_all(tri, ("dap", "ch"), split_axis=0, concat_axis=0, tiled=True)
+    tri = tri.reshape(dap, ch, slice_h, own_rows, col_span)
+    tri_full = jnp.transpose(tri, (1, 0, 2, 3, 4)).reshape(-1, own_rows, col_span)
+
     normed_out, rstd_out = normalise(tri_full.astype(jnp.float32), 0)
     gain_out = ln_out_gain.reshape(-1, 1, 1)
     bias_out = ln_out_bias.reshape(-1, 1, 1)
@@ -72,17 +85,19 @@
         jnp.einsum("ijc,hc->hij", d_proj, w_out, preferred_element_type=jnp.float32) * gain_out
     )
     d_tri = norm_backward(d_normed, normed_out, rstd_out, 0).astype(jnp.bfloat16)
-    d_split = lax.all_to_all(d_tri, "ch", split_axis=0, concat_axis=2, tiled=True)
-    d_edge_a = jnp.einsum("hij,hjk->hik", d_split, edge_b_all, preferred_element_type=jnp.float32)
-    d_edge_b = jnp.transpose(
-        lax.psum_scatter(
-            jnp.einsum("hij,hik->jhk", d_split, edge_a, preferred_element_type=jnp.float32),
-            "dap",
-            scatter_dimension=0,
-            tiled=True,
-        ),
-        (1, 0, 2),
-    )
+
+    d_tri = d_tri.reshape(ch, dap, slice_h, own_rows, col_span)
+    d_tri = jnp.transpose(d_tri, (1, 0, 2, 3, 4)).reshape(dap * ch, slice_h, own_rows, col_span)
+    d_tri = lax.all_to_all(d_tri, ("dap", "ch"), split_axis=0, concat_axis=0, tiled=True)
+    d_tri = d_tri.reshape(dap, ch, slice_h, own_rows, col_span)
+    d_tri = jnp.transpose(d_tri, (2, 0, 3, 1, 4)).reshape(slice_h, dap * own_rows, all_cols)
+    d_edge_a = jnp.einsum("hij,hjk->hik", d_tri, b_all, preferred_element_type=jnp.float32)
+    d_edge_b = jnp.einsum("hij,hik->hjk", d_tri, a_all, preferred_element_type=jnp.float32)
+    d_edges = jnp.stack((d_edge_a, d_edge_b)).astype(jnp.bfloat16)
+    d_edges = d_edges.reshape(2, slice_h, dap, own_rows, all_cols)
+    d_edges = jnp.transpose(d_edges, (2, 0, 1, 3, 4))
+    d_edges = lax.all_to_all(d_edges, "dap", split_axis=0, concat_axis=0, tiled=True)
+    d_edges = jnp.transpose(d_edges, (1, 0, 2, 3, 4)).reshape(2, hidden_local, own_rows, all_cols)
 
     def split_grad(d_edge, sig_val, proj_val):
         masked = d_edge * row_mask
@@ -92,13 +107,16 @@
         )
 
     d_four = jnp.concatenate(
-        split_grad(d_edge_a, a_sig, a_proj) + split_grad(d_edge_b, b_sig, b_proj), axis=0
+        split_grad(d_edges[0].astype(jnp.float32), a_sig, a_proj)
+        + split_grad(d_edges[1].astype(jnp.float32), b_sig, b_proj),
+        axis=0,
     )
     d_hidden = jnp.einsum("gik,cg->ikc", d_four, w_four, preferred_element_type=jnp.float32)
-    d_share = lax.psum_scatter(
-        d_hidden.astype(jnp.bfloat16), "ch", scatter_dimension=1, tiled=True
-    ).astype(jnp.float32)
-    d_pair_norm = d_share + jnp.einsum(
+    if ch > 1:
+        d_hidden = lax.psum_scatter(
+            d_hidden.astype(jnp.bfloat16), "ch", scatter_dimension=1, tiled=True
+        ).astype(jnp.float32)
+    d_pair_norm = d_hidden + jnp.einsum(
         "ijd,cd->ijc", d_gate, w_gate, preferred_element_type=jnp.float32
     )
     normed_cols = lax.dynamic_slice_in_dim(normed_in, col_first, col_span, 1)
@@ -108,6 +126,11 @@
 
 
 def solution(mesh):
+    sizes = dict(mesh.shape)
+
+    def program(*args):
+        return on_device(sizes["dap"], sizes["ch"], *args)
+
     in_specs = (
         P(("grp", "dap"), None, None),
         P(("grp", "dap"), "ch", None),
@@ -125,5 +148,5 @@
     )
     out_specs = P(("grp", "dap"), "ch", None)
     return jax.shard_map(
-        on_device, mesh=mesh, in_specs=in_specs, out_specs=out_specs, check_vma=False
+        program, mesh=mesh, in_specs=in_specs, out_specs=out_specs, check_vma=False
     )

time: 258 us -> 61.6 us (0.24)
  waiting for transfers between devices: 205 us -> 7.87 us
  blocking collectives: 0 us -> 40 us
  matrix products: 19.4 us -> 2.31 us
  between operations: 13.6 us -> 0.35 us
  local copies, waits for them, and re-layouts: 15 us -> 6.56 us
  starting transfers between devices: 0.04 us -> 2.71 us
    reduce_scatter x1 -> x0, waiting for transfers between devices: 142 us -> none  [on_device(): lax.psum_scatter(jnp.einsum('hij,hik->jhk', d_split, edge_a, preferred_el...]
    all_gather x1 -> x0, waiting for transfers between devices: 63.7 us -> none  [on_device(): edge_b_all = lax.all_gather(edge_b, 'dap', axis=1, tiled=True)]
    all_to_all x0 -> x3, blocking collectives: none -> 40 us  [the longest x1 17.7 us: on_device(): lax.all_to_all(edges, 'dap', split_axis=0, concat_axis=0, tiled=True)]
    dot_general x3, matrix products: 16 us -> 0.61 us  [the longest x1 0.23 us: on_device(): jnp.einsum('hij,hik->hjk', d_tri, a_all, preferred_element_type=jnp.float32)]
    dot_general x2 -> x0, local copies, waits for them, and re-layouts: 9.44 us -> none  [the longest x1 9.3 us: on_device(): jnp.einsum('hij,hik->jhk', d_split, edge_a, preferred_element_type=jnp.fl...]
    all_to_all x0 -> x1, waiting for transfers between devices: none -> 7.87 us  [on_device(): lax.all_to_all(tri, ('dap', 'ch'), split_axis=0, concat_axis=0, tiled=True)]
    all_to_all x0 -> x1, starting transfers between devices: none -> 2.71 us  [on_device(): lax.all_to_all(tri, ('dap', 'ch'), split_axis=0, concat_axis=0, tiled=True)]
  transfers between devices with their start and end apart: 2 -> 1, of which waited for: 2 -> 1; matrix products, arithmetic and copies ran while one was open for 3% -> 1% of each run, Pallas kernels for 0% -> 0%
where the time goes in v1:
time: 61.6 us; the launch traced here: 61.2 us
  blocking collectives  40 us (65%)
  waiting for transfers between devices  7.87 us (13%)
  local copies, waits for them, and re-layouts  6.56 us (11%)
  starting transfers between devices  2.71 us (4%)
  matrix products  2.31 us (4%)
  other arithmetic  1.45 us (2%)
    all_to_all x1, blocking collectives, on_device(): lax.all_to_all(edges, 'dap', split_axis=0, concat_axis=0, tiled=True)  17.7 us
    all_to_all x1, blocking collectives, on_device(): lax.all_to_all(d_edges, 'dap', split_axis=0, concat_axis=0, tiled=True)  12.3 us
    all_to_all x1, blocking collectives, on_device(): lax.all_to_all(d_tri, ('dap', 'ch'), split_axis=0, concat_axis=0, tiled=T...  9.93 us
    all_to_all x1, waiting for transfers between devices, on_device(): lax.all_to_all(tri, ('dap', 'ch'), split_axis=0, concat_axis=0, tiled=True)  7.87 us
    unnamed x29, local copies, waits for them, and re-layouts  3.91 us
    all_to_all x1, starting transfers between devices, on_device(): lax.all_to_all(tri, ('dap', 'ch'), split_axis=0, concat_axis=0, tiled=True)  2.71 us
  transfers between devices with their start and end apart: 1, of which 1 were waited for; matrix products, arithmetic and copies ran while one was open for 1% of the time, Pallas kernels for 0%

profile of v1, /device:TPU:0, one launch (start us, length us, event | category | flops | bytes accessed | tf_op | source)
XLA Modules:
  0.0 61.2 jit_solution(9218104322239923160)
XLA Ops:
  0.0 0.7 %copy-done.11 = s32[128]{0:T(128)S(1)} copy-done((s32[128]{0:T(128)S(1)}, s32[128]{0:T(128)}, u32[]{:S(2)}) %copy-start.11) | copy-done | bytes 536
  0.7 0.1 dynamic_slice.2
  0.8 0.1 broadcast_multiply_fusion
  0.8 0.9 %copy.75 = bf16[128,128]{0,1:T(8,128)(2,1)S(1)} copy(bf16[128,128]{1,0:T(8,128)(2,1)} %param.18) | data formatting | bytes 65536 | tf_op args[5]
  1.7 0.1 copy.76
  1.9 0.1 copy.77
  2.0 0.1 copy.78
  2.1 0.1 copy.74
  2.3 0.1 fusion.28
  2.4 0.6 %copy-done.8 = f32[128]{0:T(128)S(1)} copy-done((f32[128]{0:T(128)S(1)}, f32[128]{0:T(128)}, u32[]{:S(2)}) %copy-start.8) | copy-done | bytes 536
  3.0 0.0 copy-done.9
  3.0 0.4 fusion.47
  3.4 0.1 multiply_convert_fusion.6
  3.6 0.2 pad_maximum_fusion
  3.8 0.1 copy.103
  3.9 17.7 %all_to_all.20 = bf16[32,2,4,4,128]{4,2,3,1,0:T(4,128)(2,1)S(1)} all-to-all(bf16[32,2,4,4,128]{4,2,3,1,0:T(4,128)(2,1)S(1)} %copy.103), channel_id=1, replica_groups=mesh['grp'=1,'dap'=32,'ch'=1] {'dap'}, dimensions={0} | all-to-all | bytes 524288 | tf_op jit(solution)/shard_map/all_to_all | solution.py:60
  21.6 0.1 fusion.60
  21.7 0.1 copy.83
  21.7 0.1 copy.82
  21.8 0.2 convolution_convert_fusion.2
  22.0 0.7 %copy.108 = bf16[4,32,4,1,128]{4,2,0,1,3:T(4,128)(2,1)} copy(bf16[4,32,4,1,128]{4,2,1,0,3:T(4,128)(2,1)S(1)} %bitcast.71) | data formatting | bytes 262144 | tf_op jit(solution)/shard_map/reshape | solution.py:66
  22.7 2.7 %all-to-all-start.1 = ((bf16[32,4,4,128]{3,2,1,0:T(4,128)(2,1)}), bf16[32,4,4,128]{3,2,1,0:T(4,128)(2,1)S(1)}, u32[]{:S(2)}, u32[]{:S(2)}) async-start(bf16[32,4,4,128]{3,2,1,0:T(4,128)(2,1)} %bitcast.55), calls=%async_computation.1 | async-start | bytes 262144 | tf_op jit(solution)/shard_map/all_to_all | solution.py:68
  25.4 0.3 fusion.6
  25.8 7.9 %all-to-all-done.1 = bf16[32,4,4,128]{3,2,1,0:T(4,128)(2,1)S(1)} async-done(((bf16[32,4,4,128]{3,2,1,0:T(4,128)(2,1)}), bf16[32,4,4,128]{3,2,1,0:T(4,128)(2,1)S(1)}, u32[]{:S(2)}, u32[]{:S(2)}) %all-to-all-start.1) | async-done | bytes 131104 | tf_op jit(solution)/shard_map/all_to_all | solution.py:68
  33.6 0.1 convert_reduce_fusion.1
  33.8 0.1 multiply_reduce_fusion.1
  34.0 0.1 copy.86
  34.0 0.8 %copy-done.1 = bf16[4,128,128]{2,1,0:T(8,128)(2,1)S(1)} copy-done((bf16[4,128,128]{2,1,0:T(8,128)(2,1)S(1)}, bf16[4,128,128]{2,1,0:T(8,128)(2,1)}, u32[]{:S(2)}) %copy-start.1) | copy-done | bytes 131096
  34.9 0.2 fusion.59
  35.1 0.1 multiply_convert_fusion.4
  35.2 9.9 %all_to_all.21 = bf16[32,4,4,128]{3,1,2,0:T(4,128)(2,1)S(1)} all-to-all(bf16[32,4,4,128]{3,1,2,0:T(4,128)(2,1)S(1)} %copy.87), channel_id=1, replica_groups=mesh['grp'=1,'dap'=32,'ch'=1] {'dap','ch'}, dimensions={0} | all-to-all | bytes 262144 | tf_op jit(solution)/shard_map/all_to_all | solution.py:91
  45.2 0.1 copy.88
  45.2 0.2 convolution_convert_fusion
  45.5 0.2 convolution_convert_fusion.1
  45.6 0.1 copy.90
  45.8 0.1 copy.91
  45.9 0.2 maximum_bitcast_fusion
  46.0 12.3 %all_to_all.22 = bf16[32,2,4,4,128]{4,2,3,1,0:T(4,128)(2,1)S(1)} all-to-all(bf16[32,2,4,4,128]{4,2,3,1,0:T(4,128)(2,1)S(1)} %maximum_bitcast_fusion), channel_id=1, replica_groups=mesh['grp'=1,'dap'=32,'ch'=1] {'dap'}, dimensions={0} | all-to-all | bytes 524288 | tf_op jit(solution)/shard_map/all_to_all | solution.py:99
  58.4 0.1 copy.107
  58.5 0.1 slice_convert_fusion.1
  58.6 0.2 copy.93
  58.7 0.2 copy.94
  58.9 0.2 multiply_convert_fusion.3
  59.2 0.3 fusion.8
  59.5 0.4 copy-done.10
  59.8 0.5 fusion.58
  60.4 0.1 fusion.27
  60.5 0.8 %copy.97 = bf16[4,128,128]{2,1,0:T(8,128)(2,1)} copy(bf16[4,128,128]{1,2,0:T(8,128)(2,1)S(1)} %fusion.27) | data formatting | bytes 262144 | tf_op jit(solution)/shard_map/convert_element_type | solution.py:125
  (29 shorter events, 0.2 us)
Async XLA Ops:
  0.0 34.0 %copy-start = (bf16[128,128]{1,0:T(8,128)(2,1)S(1)}, bf16[128,128]{1,0:T(8,128)(2,1)}, u32[]{:S(2)}) copy-start(bf16[128,128]{1,0:T(8,128)(2,1)} %param.25) | copy-start | bytes 98308
  0.0 0.7 %copy-start.11 = (s32[128]{0:T(128)S(1)}, s32[128]{0:T(128)}, u32[]{:S(2)}) copy-start(s32[128]{0:T(128)} %param.15) | copy-start | bytes 1540
  0.7 1.0 %copy-start.4 = (bf16[128,128]{1,0:T(8,128)(2,1)S(1)}, bf16[128,128]{1,0:T(8,128)(2,1)}, u32[]{:S(2)}) copy-start(bf16[128,128]{1,0:T(8,128)(2,1)} %param.19) | copy-start | bytes 98308
  0.7 1.1 %copy-start.5 = (bf16[128,128]{1,0:T(8,128)(2,1)S(1)}, bf16[128,128]{1,0:T(8,128)(2,1)}, u32[]{:S(2)}) copy-start(bf16[128,128]{1,0:T(8,128)(2,1)} %param.20) | copy-start | bytes 98308
  0.8 1.2 %copy-start.6 = (bf16[128,128]{1,0:T(8,128)(2,1)S(1)}, bf16[128,128]{1,0:T(8,128)(2,1)}, u32[]{:S(2)}) copy-start(bf16[128,128]{1,0:T(8,128)(2,1)} %param.21) | copy-start | bytes 98308
  0.8 1.3 %copy-start.2 = (bf16[4,128,128]{2,1,0:T(8,128)(2,1)S(1)}, bf16[4,128,128]{2,1,0:T(8,128)(2,1)}, u32[]{:S(2)}) copy-start(bf16[4,128,128]{2,1,0:T(8,128)(2,1)} %param.13) | copy-start | bytes 393220
  2.4 0.7 %copy-start.8 = (f32[128]{0:T(128)S(1)}, f32[128]{0:T(128)}, u32[]{:S(2)}) copy-start(f32[128]{0:T(128)} %param.16) | copy-start | bytes 1540
  2.4 0.7 %copy-start.9 = (f32[128]{0:T(128)S(1)}, f32[128]{0:T(128)}, u32[]{:S(2)}) copy-start(f32[128]{0:T(128)} %param.17) | copy-start | bytes 1540
  22.7 2.7 %copy-start.3 = (bf16[128,128]{1,0:T(8,128)(2,1)S(1)}, bf16[128,128]{1,0:T(8,128)(2,1)}, u32[]{:S(2)}) copy-start(bf16[128,128]{1,0:T(8,128)(2,1)} %param.22) | copy-start | bytes 98308
  22.7 10.9 %all-to-all-start.1 = ((bf16[32,4,4,128]{3,2,1,0:T(4,128)(2,1)}), bf16[32,4,4,128]{3,2,1,0:T(4,128)(2,1)S(1)}, u32[]{:S(2)}, u32[]{:S(2)}) async-start(bf16[32,4,4,128]{3,2,1,0:T(4,128)(2,1)} %bitcast.55), calls=%async_computation.1 | async-start | bytes 262144 | tf_op jit(solution)/shard_map/all_to_all | solution.py:68
  33.9 0.9 %copy-start.1 = (bf16[4,128,128]{2,1,0:T(8,128)(2,1)S(1)}, bf16[4,128,128]{2,1,0:T(8,128)(2,1)}, u32[]{:S(2)}) copy-start(bf16[4,128,128]{2,1,0:T(8,128)(2,1)} %param.14) | copy-start | bytes 393220
  34.0 0.8 %copy-start.7 = (f32[128]{0:T(128)S(1)}, f32[128]{0:T(128)}, u32[]{:S(2)}) copy-start(f32[128]{0:T(128)} %param.23) | copy-start | bytes 1540
  59.2 0.7 %copy-start.10 = (f32[128]{0:T(128)S(1)}, f32[128]{0:T(128)}, u32[]{:S(2)}) copy-start(f32[128]{0:T(128)} %param.24) | copy-start | bytes 1540

commit v2 on v1

--- a/solution.py
+++ b/solution.py
@@ -18,7 +18,7 @@
     return inverse * (grad_hat - mean_grad - normed * mean_proj)
 
 
-def on_device(
+def channel_shards(
     dap,
     ch,
     pair_act,
@@ -125,11 +125,115 @@
     return norm_backward(grad_hat, normed_cols, rstd_cols, 2).astype(jnp.bfloat16)
 
 
+def gather_tiles(
+    dap,
+    pair_act,
+    out_grad,
+    residue_mask,
+    ln_in_gain,
+    ln_in_bias,
+    w_a_proj,
+    w_a_gate,
+    w_b_proj,
+    w_b_gate,
+    w_gate,
+    ln_out_gain,
+    ln_out_bias,
+    w_out,
+):
+    own, cols, chan = pair_act.shape
+    plane = 1 << ((dap.bit_length()) // 2)
+    column = dap // plane
+    me = lax.axis_index("dap")
+    place, level = me % plane, me // plane
+    span = plane * own
+
+    def send(value, mask):
+        return lax.ppermute(value, "dap", [(i, i ^ mask) for i in range(dap)])
+
+    row_acts = [pair_act] + [send(pair_act, t * plane) for t in range(1, column)]
+    col_acts = [pair_act] + [send(pair_act, s) for s in range(1, plane)]
+    grads = []
+    for t in range(column):
+        part = lax.dynamic_slice_in_dim(out_grad, (level ^ t) * span, span, 1)
+        grads.append(send(part, t * plane) if t else part)
+    upstream = jnp.concatenate(grads, axis=0).astype(jnp.float32)
+    row_act = jnp.concatenate(row_acts, axis=0)
+    col_act = jnp.concatenate(col_acts, axis=0)
+    valid = residue_mask.astype(jnp.float32)
+    ids_row = jnp.concatenate([(me ^ (t * plane)) * own + jnp.arange(own) for t in range(column)])
+    ids_col = jnp.concatenate([(me ^ s) * own + jnp.arange(own) for s in range(plane)])
+
+    def edges(act, ids, w_proj, w_sig):
+        normed, _ = normalise(act.astype(jnp.float32), 2)
+        pair_norm = (normed * ln_in_gain + ln_in_bias).astype(jnp.bfloat16)
+        proj = jnp.einsum("ikc,ch->hik", pair_norm, w_proj, preferred_element_type=jnp.float32)
+        sig = jax.nn.sigmoid(
+            jnp.einsum("ikc,ch->hik", pair_norm, w_sig, preferred_element_type=jnp.float32)
+        )
+        mask = valid[ids][:, None] * valid[None, :]
+        return pair_norm, proj, sig, mask, (mask * sig * proj).astype(jnp.bfloat16)
+
+    norm_a, a_proj, a_sig, mask_a, edge_a = edges(row_act, ids_row, w_a_proj, w_a_gate)
+    _, b_proj, b_sig, mask_b, edge_b = edges(col_act, ids_col, w_b_proj, w_b_gate)
+    order = jnp.bitwise_xor(place, jnp.arange(plane))
+
+    def to_slots(value):
+        value = value.reshape(value.shape[0], plane, own, chan)
+        return jnp.take(value, order, axis=1).reshape(-1, span, chan)
+
+    tri = jnp.einsum("hik,hjk->hij", edge_a, edge_b, preferred_element_type=jnp.float32)
+    normed_out, rstd_out = normalise(tri.astype(jnp.bfloat16).astype(jnp.float32), 0)
+    gain_out = ln_out_gain.reshape(-1, 1, 1)
+    tri_norm = (normed_out * gain_out + ln_out_bias.reshape(-1, 1, 1)).astype(jnp.bfloat16)
+    proj_out = jnp.einsum("hij,hc->ijc", tri_norm, w_out, preferred_element_type=jnp.float32)
+    norm_tile = to_slots(lax.dynamic_slice_in_dim(norm_a, level * span, span, 1))
+    upstream = to_slots(upstream)
+    gate_act = jax.nn.sigmoid(
+        jnp.einsum("ijc,cd->ijd", norm_tile, w_gate, preferred_element_type=jnp.float32)
+    )
+    d_proj = (upstream * gate_act).astype(jnp.bfloat16)
+    d_gate = (upstream * proj_out * gate_act * (1.0 - gate_act)).astype(jnp.bfloat16)
+    d_normed = (
+        jnp.einsum("ijc,hc->hij", d_proj, w_out, preferred_element_type=jnp.float32) * gain_out
+    )
+    d_tri = norm_backward(d_normed, normed_out, rstd_out, 0).astype(jnp.bfloat16)
+    d_edge_a = jnp.einsum("hij,hjk->hik", d_tri, edge_b, preferred_element_type=jnp.float32)
+    d_edge_b = jnp.einsum("hij,hik->hjk", d_tri, edge_a, preferred_element_type=jnp.float32)
+
+    def back(d_edge, mask, sig, proj, w_proj, w_sig):
+        masked = d_edge * mask * sig
+        d_proj_in = masked.astype(jnp.bfloat16)
+        d_sig_in = (masked * proj * (1.0 - sig)).astype(jnp.bfloat16)
+        both = jnp.concatenate((d_proj_in, d_sig_in), axis=0)
+        weights = jnp.concatenate((w_proj, w_sig), axis=1)
+        return jnp.einsum("gik,cg->ikc", both, weights, preferred_element_type=jnp.float32)
+
+    share_b = back(d_edge_b, mask_b, b_sig, b_proj, w_b_proj, w_b_gate).astype(jnp.bfloat16)
+    share_a = back(d_edge_a, mask_a, a_sig, a_proj, w_a_proj, w_a_gate)
+    gate_part = jnp.einsum("ijd,cd->ijc", d_gate, w_gate, preferred_element_type=jnp.float32)
+    gate_part = to_slots(gate_part)
+    old = lax.dynamic_slice_in_dim(share_a, level * span, span, 1)
+    share_a = lax.dynamic_update_slice_in_dim(share_a, old + gate_part, level * span, 1)
+    share_a = share_a.astype(jnp.bfloat16)
+    total = jnp.zeros(pair_act.shape, jnp.float32)
+    for t in range(column):
+        part = share_a[t * own : (t + 1) * own]
+        total = total + (send(part, t * plane) if t else part).astype(jnp.float32)
+    for s in range(plane):
+        part = share_b[s * own : (s + 1) * own]
+        total = total + (send(part, s) if s else part).astype(jnp.float32)
+    normed_in, rstd_in = normalise(pair_act.astype(jnp.float32), 2)
+    return norm_backward(total * ln_in_gain, normed_in, rstd_in, 2).astype(jnp.bfloat16)
+
+
 def solution(mesh):
     sizes = dict(mesh.shape)
 
     def program(*args):
-        return on_device(sizes["dap"], sizes["ch"], *args)
+        if sizes["ch"] == 1 and sizes["dap"] & (sizes["dap"] - 1) == 0:
+            return gather_tiles(sizes["dap"], *args)
+        return channel_shards(sizes["dap"], sizes["ch"], *args)
 
     in_specs = (
         P(("grp", "dap"), None, None),

time: 61.6 us -> 86.7 us (1.41)
  blocking collectives: 40 us -> 0 us
  starting transfers between devices: 2.71 us -> 31.2 us
  waiting for transfers between devices: 7.87 us -> 20.1 us
  matrix products: 2.31 us -> 13.9 us
  other arithmetic: 1.45 us -> 12.7 us
  local copies, waits for them, and re-layouts: 6.56 us -> 7.65 us
    all_to_all x3 -> x0, blocking collectives: 40 us -> none  [the longest x1 17.7 us: on_device(): lax.all_to_all(edges, 'dap', split_axis=0, concat_axis=0, tiled=True)]
    ppermute x0 -> x23, starting transfers between devices: none -> 31.2 us  [send(): return lax.ppermute(value, 'dap', [(i, i ^ mask) for i in range(dap)])]
    ppermute x0 -> x23, waiting for transfers between devices: none -> 20.1 us  [send(): return lax.ppermute(value, 'dap', [(i, i ^ mask) for i in range(dap)])]
    dot_general x8 -> x12, matrix products: 2.31 us -> 13.9 us  [the longest x2 4.06 us: edges(): jnp.einsum('ikc,ch->hik', pair_norm, w_proj, preferred_element_type=jnp.f...]
    all_to_all x1 -> x0, waiting for transfers between devices: 7.87 us -> none  [on_device(): lax.all_to_all(tri, ('dap', 'ch'), split_axis=0, concat_axis=0, tiled=True)]
    convert_element_type x6 -> x8, other arithmetic: 0.61 us -> 6.35 us  [the longest x2 3.45 us: back(): d_proj_in = masked.astype(jnp.bfloat16)]
    gather x0 -> x5, local copies, waits for them, and re-layouts: none -> 3.18 us  [the longest x3 1.83 us: to_slots(): return jnp.take(value, order, axis=1).reshape(-1, span, chan)]
    all_to_all x1 -> x0, starting transfers between devices: 2.71 us -> none  [on_device(): lax.all_to_all(tri, ('dap', 'ch'), split_axis=0, concat_axis=0, tiled=True)]
  transfers between devices with their start and end apart: 1 -> 23, of which waited for: 1 -> 6; matrix products, arithmetic and copies ran while one was open for 1% -> 14% of each run, Pallas kernels for 0% -> 0%
where the time goes in v2:
time: 86.7 us; the launch traced here: 86.4 us
  starting transfers between devices  31.2 us (36%)
  waiting for transfers between devices  20.1 us (23%)
  matrix products  13.9 us (16%)
  other arithmetic  12.7 us (15%)
  local copies, waits for them, and re-layouts  7.65 us (9%)
    ppermute x23, starting transfers between devices, send(): return lax.ppermute(value, 'dap', [(i, i ^ mask) for i in range(dap)])  31.2 us
    ppermute x23, waiting for transfers between devices, send(): return lax.ppermute(value, 'dap', [(i, i ^ mask) for i in range(dap)])  20.1 us
    dot_general x2, matrix products, edges(): jnp.einsum('ikc,ch->hik', pair_norm, w_proj, preferred_element_type=jnp.f...  4.06 us
    convert_element_type x2, other arithmetic, back(): d_proj_in = masked.astype(jnp.bfloat16)  3.45 us
    reduce_sum x4, other arithmetic, normalise(): jnp.mean(centre * centre, axis=reduce_dim, keepdims=True) + EPSILON  2.42 us
    dot_general x2, matrix products, edges(): jnp.einsum('ikc,ch->hik', pair_norm, w_sig, preferred_element_type=jnp.fl...  1.91 us
    dot_general x1, matrix products, gather_tiles(): jnp.einsum('hij,hik->hjk', d_tri, edge_a, preferred_element_type=jnp.floa...  1.89 us
    gather x3, local copies, waits for them, and re-layouts, to_slots(): return jnp.take(value, order, axis=1).reshape(-1, span, chan)  1.83 us
  transfers between devices with their start and end apart: 23, of which 6 were waited for; matrix products, arithmetic and copies ran while one was open for 14% of the time, Pallas kernels for 0%

profile of v2, /device:TPU:0, one launch (start us, length us, event | category | flops | bytes accessed | tf_op | source)
XLA Modules:
  0.0 86.4 jit_solution(2253460092606241417)
XLA Ops:
  0.5 2.6 %collective-permute-start.4 = (bf16[4,128,128]{2,1,0:T(8,128)(2,1)}, bf16[4,128,128]{2,1,0:T(8,128)(2,1)S(1)}, u32[]{:S(2)}, u32[]{:S(2)}) collective-permute-start(bf16[4,128,128]{2,1,0:T(8,128)(2,1)} %param.15), channel_id=1, source_target_pairs={{0,2},{1,3},{2,0},{3,1},{4,6},{5,7},{6,4},{7,5},{8,10},{9,11},{10,... | collective-permute-start | bytes 393224 | tf_op jit(solution)/shard_map/ppermute | solution.py:152
  3.0 0.8 constant_dynamic-slice_fusion.4
  3.8 1.6 %collective-permute-start.10 = (bf16[4,32,128]{2,1,0:T(8,128)(2,1)S(1)}, bf16[4,32,128]{2,1,0:T(8,128)(2,1)S(1)}, u32[]{:S(2)}, u32[]{:S(2)}) collective-permute-start(bf16[4,32,128]{2,1,0:T(8,128)(2,1)S(1)} %get-tuple-element.26), channel_id=1, source_target_pairs={{0,8},{1,9},{2,10},{3,11},{4,12},{5,13},{6,14},{7,15},{8,0},{9,1},... | collective-permute-start | bytes 98312 | tf_op jit(solution)/shard_map/ppermute | solution.py:152
  5.5 2.6 %collective-permute-start.11 = (bf16[4,32,128]{2,1,0:T(8,128)(2,1)S(1)}, bf16[4,32,128]{2,1,0:T(8,128)(2,1)S(1)}, u32[]{:S(2)}, u32[]{:S(2)}) collective-permute-start(bf16[4,32,128]{2,1,0:T(8,128)(2,1)S(1)} %get-tuple-element.28), channel_id=1, source_target_pairs={{0,16},{1,17},{2,18},{3,19},{4,20},{5,21},{6,22},{7,23},{8,24},{9,... | collective-permute-start | bytes 98312 | tf_op jit(solution)/shard_map/ppermute | solution.py:152
  8.3 0.9 %constant_dynamic-update-slice_fusion.7 = bf16[32,128,128]{2,1,0:T(8,128)(2,1)S(1)} fusion(bf16[4,128,128]{2,1,0:T(8,128)(2,1)} %param.15), kind=kLoop, calls=%fused_computation.133 | loop fusion | bytes 262144
  9.2 1.0 %convert_reduce_fusion.3 = f32[4,128]{1,0:T(4,128)S(1)} fusion(bf16[4,128,128]{2,1,0:T(8,128)(2,1)} %param.15), kind=kLoop, calls=%fused_computation.75 | loop fusion | flops 130560 | bytes 133120 | tf_op jit(solution)/shard_map/reduce_sum | solution.py:10
  10.5 0.7 convert_element_type.104
  11.1 0.7 gather_fusion.1
  12.0 0.7 gather_fusion
  12.7 0.6 pad_clamp_fusion
  13.5 0.6 broadcast_in_dim.18
  14.1 1.6 %collective-permute-start.6 = (bf16[4,128,128]{2,1,0:T(8,128)(2,1)}, bf16[4,128,128]{2,1,0:T(8,128)(2,1)S(1)}, u32[]{:S(2)}, u32[]{:S(2)}) collective-permute-start(bf16[4,128,128]{2,1,0:T(8,128)(2,1)} %param.15), channel_id=1, source_target_pairs={{0,4},{1,5},{2,6},{3,7},{4,0},{5,1},{6,2},{7,3},{8,12},{9,13},{10,... | collective-permute-start | bytes 393224 | tf_op jit(solution)/shard_map/ppermute | solution.py:152
  16.2 0.6 gather_fusion.3
  17.0 2.7 %collective-permute-start.8 = (bf16[4,128,128]{2,1,0:T(8,128)(2,1)S(1)}, bf16[4,128,128]{2,1,0:T(8,128)(2,1)S(1)}, u32[]{:S(2)}, u32[]{:S(2)}) collective-permute-start(bf16[4,128,128]{2,1,0:T(8,128)(2,1)S(1)} %copy-done.1), channel_id=1, source_target_pairs={{0,6},{1,7},{2,4},{3,5},{4,2},{5,3},{6,0},{7,1},{8,14},{9,15},{10,... | collective-permute-start | bytes 393224 | tf_op jit(solution)/shard_map/ppermute | solution.py:152
  19.8 0.7 collective-permute-start
  20.7 3.5 %collective-permute-start.1 = (bf16[4,128,128]{2,1,0:T(8,128)(2,1)S(1)}, bf16[4,128,128]{2,1,0:T(8,128)(2,1)S(1)}, u32[]{:S(2)}, u32[]{:S(2)}) collective-permute-start(bf16[4,128,128]{2,1,0:T(8,128)(2,1)S(1)} %copy-done.1), channel_id=1, source_target_pairs={{0,16},{1,17},{2,18},{3,19},{4,20},{5,21},{6,22},{7,23},{8,24},{9,... | collective-permute-start | bytes 393224 | tf_op jit(solution)/shard_map/ppermute | solution.py:152
  24.2 4.0 %collective-permute-done.7 = bf16[4,128,128]{2,1,0:T(8,128)(2,1)S(1)} collective-permute-done((bf16[4,128,128]{2,1,0:T(8,128)(2,1)S(1)}, bf16[4,128,128]{2,1,0:T(8,128)(2,1)S(1)}, u32[]{:S(2)}, u32[]{:S(2)}) %collective-permute-start.7) | collective-permute-done | bytes 131104 | tf_op jit(solution)/shard_map/ppermute | solution.py:152
  28.2 3.9 %collective-permute-start.2 = (bf16[4,128,128]{2,1,0:T(8,128)(2,1)S(1)}, bf16[4,128,128]{2,1,0:T(8,128)(2,1)S(1)}, u32[]{:S(2)}, u32[]{:S(2)}) collective-permute-start(bf16[4,128,128]{2,1,0:T(8,128)(2,1)S(1)} %copy-done.1), channel_id=1, source_target_pairs={{0,24},{1,25},{2,26},{3,27},{4,28},{5,29},{6,30},{7,31},{8,16},{9,... | collective-permute-start | bytes 393224 | tf_op jit(solution)/shard_map/ppermute | solution.py:152
  32.6 1.3 %fusion.2 = f32[32,128]{1,0:T(8,128)S(1)} fusion(bf16[32,128,128]{2,1,0:T(8,128)(2,1)S(1)} %constant_dynamic-update-slice_fusion, f32[32,128]{1,0:T(8,128)S(1)} %broadcast_multiply_fusion), kind=kLoop, calls=%fused_computation.9 | loop fusion | flops 2093056 | bytes 1081344 | tf_op jit(solution)/shard_map/reduce_sum | solution.py:11
  33.9 2.4 %collective-permute-done.2 = bf16[4,128,128]{2,1,0:T(8,128)(2,1)S(1)} collective-permute-done((bf16[4,128,128]{2,1,0:T(8,128)(2,1)S(1)}, bf16[4,128,128]{2,1,0:T(8,128)(2,1)S(1)}, u32[]{:S(2)}, u32[]{:S(2)}) %collective-permute-start.2) | collective-permute-done | bytes 131104 | tf_op jit(solution)/shard_map/ppermute | solution.py:152
  36.6 0.6 fusion.31
  37.2 0.7 fusion.34
  38.0 0.5 fusion.20
  38.8 1.4 %add_divide_fusion = f32[32,128,128]{1,2,0:T(8,128)S(1)} fusion(bf16[32,128,128]{2,1,0:T(8,128)(2,1)S(1)} %constant_dynamic-update-slice_fusion, f32[128]{0:T(128)S(1)} %copy-done.18, f32[128]{0:T(128)S(1)} %copy-done.14, f32[32,128]{1,0:T(8,128)S(1)} %add_rsqrt_fusion, f32[32,128]{1,0:T(8,128)S(1)} %broadcast_multiply_fusion, ...), kind=kOutput, calls=%fused_computation.26 | convolution fusion | flops 138936320 | bytes 3212288 | tf_op jit(solution)/shard_map/ikc,ch->hik/dot_general | solution.py:172
  40.2 2.7 %fusion.10 = (bf16[128,32,128]{2,0,1:T(8,128)(2,1)S(1)}, f32[32,128,128]{1,2,0:T(8,128)}) fusion(f32[32,128,128]{1,2,0:T(8,128)S(1)} %add_divide_fusion, f32[32,128]{1,0:T(8,128)S(1)} %broadcast_multiply_fusion.1, bf16[128,128]{1,0:T(8,128)(2,1)S(1)} %copy-done.11, bf16[32,128,128]{2,1,0:T(8,128)(2,1)S(1)} %constant_dynamic-update-slice_fusion, ...), kind=kOutput, calls=%fused_computation.19 | convolution fusion | flops 138936320 | bytes 6374400 | tf_op jit(solution)/shard_map/ikc,ch->hik/dot_general | solution.py:170
  42.9 1.4 %multiply_convert_fusion.1 = (bf16[128,16,128]{2,0,1:T(8,128)(2,1)S(1)}, f32[128,16,128]{2,0,1:T(8,128)}) fusion(f32[128,16,128]{2,0,1:T(8,128)S(1)} %fusion.20, f32[16,128]{1,0:T(8,128)S(1)} %broadcast_multiply_fusion.6, bf16[16,128,128]{2,1,0:T(8,128)(2,1)S(1)} %fusion.34, bf16[128,128]{1,0:T(8,128)(2,1)S(1)} %copy-done.9), kind=kOutput, calls=%fused_computation.61 | convolution fusion | flops 67895296 | bytes 3186688 | tf_op jit(solution)/shard_map/ikc,ch->hik/dot_general | solution.py:170
  44.3 1.0 %fusion.42 = bf16[128,16,32]{2,1,0:T(8,128)(2,1)S(1)} fusion(bf16[128,32,128]{2,0,1:T(8,128)(2,1)S(1)} %get-tuple-element.29, bf16[128,16,128]{2,0,1:T(8,128)(2,1)S(1)} %get-tuple-element.31), kind=kOutput, calls=%fused_computation.64 | convolution fusion | flops 16777216 | bytes 1703936 | tf_op jit(solution)/shard_map/hik,hjk->hij/dot_general | solution.py:185
  45.3 0.5 copy.55
  46.3 0.7 gather_fusion.2
  48.5 1.8 %fusion.40 = f32[128,16,128]{2,1,0:T(8,128)} fusion(bf16[128,16,32]{2,1,0:T(8,128)(2,1)S(1)} %copy.63, bf16[128,32,128]{2,0,1:T(8,128)(2,1)S(1)} %get-tuple-element.29), kind=kOutput, calls=%fused_computation.62 | convolution fusion | flops 16777216 | bytes 2228224 | tf_op jit(solution)/shard_map/hij,hjk->hik/dot_general | solution.py:201
  50.3 1.9 %fusion.48 = f32[128,32,128]{2,1,0:T(8,128)} fusion(bf16[128,16,32]{2,1,0:T(8,128)(2,1)S(1)} %copy.63, bf16[128,16,128]{2,0,1:T(8,128)(2,1)S(1)} %get-tuple-element.31), kind=kOutput, calls=%fused_computation.69 | convolution fusion | flops 16777216 | bytes 2752512 | tf_op jit(solution)/shard_map/hij,hik->hjk/dot_general | solution.py:202
  52.2 1.4 %fusion.30 = f32[16,32,128]{2,1,0:T(8,128)S(1)} fusion(f32[16,32,128]{2,1,0:T(8,128)S(1)} %fusion.28, f32[16,32,128]{2,1,0:T(8,128)S(1)} %bitcast.110, bf16[128,16,32]{0,2,1:T(8,128)(2,1)S(1)} %copy.55, f32[128]{0:T(128)} %param.26, f32[128]{0:T(128)} %param.25, f32[16,32]{1,0:T(8,128)S(1)} %add_rsqrt_fusion.1, f32[16,32]{1,0:T(8,128)S(1)} %broadcast_multiply_fusion.4, ...), kind=kOutput, calls=%fused_computation.49 | convolution fusion | flops 34275328 | bytes 988160 | tf_op jit(solution)/shard_map/ijd,cd->ijc/dot_general | solution.py:214
  53.7 0.6 gather_fusion.4
  54.3 0.7 select_bitcast_fusion
  55.1 1.9 %fusion.47 = (bf16[128,16,128]{2,0,1:T(8,128)(2,1)S(1)}, bf16[128,16,128]{2,0,1:T(8,128)(2,1)S(1)}) fusion(f32[128,16,128]{2,0,1:T(8,128)S(1)} %copy-done.7, f32[16,128]{1,0:T(8,128)S(1)} %broadcast_multiply_fusion.6, f32[128,16,128]{2,1,0:T(8,128)} %fusion.40, f32[128,16,128]{2,0,1:T(8,128)S(1)} %copy-done.8), kind=kLoop, calls=%fused_computation.68 | loop fusion | flops 1835008 | bytes 4202496 | tf_op jit(solution)/shard_map/convert_element_type | solution.py:206
  57.0 0.5 fusion.35
  57.7 1.6 %collective-permute-start.13 = (bf16[4,128,128]{2,1,0:T(8,128)(2,1)S(1)}, bf16[4,128,128]{2,1,0:T(8,128)(2,1)S(1)}, u32[]{:S(2)}, u32[]{:S(2)}) collective-permute-start(bf16[4,128,128]{2,1,0:T(8,128)(2,1)S(1)} %get-tuple-element.22), channel_id=1, source_target_pairs={{0,8},{1,9},{2,10},{3,11},{4,12},{5,13},{6,14},{7,15},{8,0},{9,1},... | collective-permute-start | bytes 393224 | tf_op jit(solution)/shard_map/ppermute | solution.py:152
  59.3 2.5 %collective-permute-start.14 = (bf16[4,128,128]{2,1,0:T(8,128)(2,1)S(1)}, bf16[4,128,128]{2,1,0:T(8,128)(2,1)S(1)}, u32[]{:S(2)}, u32[]{:S(2)}) collective-permute-start(bf16[4,128,128]{2,1,0:T(8,128)(2,1)S(1)} %get-tuple-element.24), channel_id=1, source_target_pairs={{0,16},{1,17},{2,18},{3,19},{4,20},{5,21},{6,22},{7,23},{8,24},{9,... | collective-permute-start | bytes 393224 | tf_op jit(solution)/shard_map/ppermute | solution.py:152
  62.2 1.6 %fusion.13 = (bf16[128,32,128]{2,0,1:T(8,128)(2,1)S(1)}, bf16[128,32,128]{2,0,1:T(8,128)(2,1)S(1)}) fusion(f32[32,128,128]{1,2,0:T(8,128)S(1)} %copy-done.3, f32[128,32,128]{2,1,0:T(8,128)S(1)} %copy-done.5, f32[32,128]{1,0:T(8,128)S(1)} %broadcast_multiply_fusion.1, f32[32,128,128]{1,2,0:T(8,128)S(1)} %copy-done.4), kind=kLoop, calls=%fused_computation.27 | loop fusion | flops 3670016 | bytes 8404992 | tf_op jit(solution)/shard_map/convert_element_type | solution.py:206
  63.8 0.8 fusion.14
  64.7 1.2 %collective-permute-start.17 = (bf16[4,128,128]{2,1,0:T(8,128)(2,1)S(1)}, bf16[4,128,128]{2,1,0:T(8,128)(2,1)S(1)}, u32[]{:S(2)}, u32[]{:S(2)}) collective-permute-start(bf16[4,128,128]{2,1,0:T(8,128)(2,1)S(1)} %get-tuple-element.21), channel_id=1, source_target_pairs={{0,2},{1,3},{2,0},{3,1},{4,6},{5,7},{6,4},{7,5},{8,10},{9,11},{10,... | collective-permute-start | bytes 393224 | tf_op jit(solution)/shard_map/ppermute | solution.py:152
  66.2 0.7 collective-permute-start.18
  66.9 5.1 %collective-permute-done.14 = bf16[4,128,128]{2,1,0:T(8,128)(2,1)S(1)} collective-permute-done((bf16[4,128,128]{2,1,0:T(8,128)(2,1)S(1)}, bf16[4,128,128]{2,1,0:T(8,128)(2,1)S(1)}, u32[]{:S(2)}, u32[]{:S(2)}) %collective-permute-start.14) | collective-permute-done | bytes 131104 | tf_op jit(solution)/shard_map/ppermute | solution.py:152
  72.0 1.5 %collective-permute-start.19 = (bf16[4,128,128]{2,1,0:T(8,128)(2,1)S(1)}, bf16[4,128,128]{2,1,0:T(8,128)(2,1)S(1)}, u32[]{:S(2)}, u32[]{:S(2)}) collective-permute-start(bf16[4,128,128]{2,1,0:T(8,128)(2,1)S(1)} %get-tuple-element.19), channel_id=1, source_target_pairs={{0,4},{1,5},{2,6},{3,7},{4,0},{5,1},{6,2},{7,3},{8,12},{9,13},{10,... | collective-permute-start | bytes 393224 | tf_op jit(solution)/shard_map/ppermute | solution.py:152
  73.8 2.6 %collective-permute-start.22 = (bf16[4,128,128]{2,1,0:T(8,128)(2,1)S(1)}, bf16[4,128,128]{2,1,0:T(8,128)(2,1)S(1)}, u32[]{:S(2)}, u32[]{:S(2)}) collective-permute-start(bf16[4,128,128]{2,1,0:T(8,128)(2,1)S(1)} %get-tuple-element.16), channel_id=1, source_target_pairs={{0,7},{1,6},{2,5},{3,4},{4,3},{5,2},{6,1},{7,0},{8,15},{9,14},{10,... | collective-permute-start | bytes 393224 | tf_op jit(solution)/shard_map/ppermute | solution.py:152
  76.5 6.6 %collective-permute-done.19 = bf16[4,128,128]{2,1,0:T(8,128)(2,1)S(1)} collective-permute-done((bf16[4,128,128]{2,1,0:T(8,128)(2,1)S(1)}, bf16[4,128,128]{2,1,0:T(8,128)(2,1)S(1)}, u32[]{:S(2)}, u32[]{:S(2)}) %collective-permute-start.19) | collective-permute-done | bytes 131104 | tf_op jit(solution)/shard_map/ppermute | solution.py:152
  83.0 1.9 %collective-permute-done.20 = bf16[4,128,128]{2,1,0:T(8,128)(2,1)S(1)} collective-permute-done((bf16[4,128,128]{2,1,0:T(8,128)(2,1)S(1)}, bf16[4,128,128]{2,1,0:T(8,128)(2,1)S(1)}, u32[]{:S(2)}, u32[]{:S(2)}) %collective-permute-start.20) | collective-permute-done | bytes 131104 | tf_op jit(solution)/shard_map/ppermute | solution.py:152
  85.4 1.0 %fusion.63 = bf16[4,128,128]{2,1,0:T(8,128)(2,1)} fusion(bf16[4,128,128]{2,1,0:T(8,128)(2,1)S(1)} %copy-done.1, f32[4,128,128]{2,1,0:T(8,128)S(1)} %get-tuple-element.10, f32[4,128]{1,0:T(4,128)S(1)} %broadcast_multiply_fusion.7, f32[4,128]{1,0:T(4,128)S(1)} %broadcast_multiply_fusion.8, f32[4,128]{1,0:T(4,128)S(1)} %add_rsqrt_fusion.3, ...), kind=kLoop, calls=%fused_computation.88 | loop fusion | flops 524288 | bytes 532480 | tf_op jit(solution)/shard_map/convert_element_type | solution.py:227
  (132 shorter events, 6.9 us)
Async XLA Ops:
  0.0 47.3 %copy-start = (bf16[128,128]{1,0:T(8,128)(2,1)S(1)}, bf16[128,128]{1,0:T(8,128)(2,1)}, u32[]{:S(2)}) copy-start(bf16[128,128]{1,0:T(8,128)(2,1)} %param.27) | copy-start | bytes 98308
  0.0 15.7 %copy-start.1 = (bf16[4,128,128]{2,1,0:T(8,128)(2,1)S(1)}, bf16[4,128,128]{2,1,0:T(8,128)(2,1)}, u32[]{:S(2)}) copy-start(bf16[4,128,128]{2,1,0:T(8,128)(2,1)} %param.15) | copy-start | bytes 393220
  0.0 16.9 %collective-permute-start.3 = (bf16[4,128,128]{2,1,0:T(8,128)(2,1)}, bf16[4,128,128]{2,1,0:T(8,128)(2,1)S(1)}, u32[]{:S(2)}, u32[]{:S(2)}) collective-permute-start(bf16[4,128,128]{2,1,0:T(8,128)(2,1)} %param.15), channel_id=1, source_target_pairs={{0,1},{1,0},{2,3},{3,2},{4,5},{5,4},{6,7},{7,6},{8,9},{9,8},{10,11... | collective-permute-start | bytes 393224 | tf_op jit(solution)/shard_map/ppermute | solution.py:152
  0.5 19.2 %collective-permute-start.4 = (bf16[4,128,128]{2,1,0:T(8,128)(2,1)}, bf16[4,128,128]{2,1,0:T(8,128)(2,1)S(1)}, u32[]{:S(2)}, u32[]{:S(2)}) collective-permute-start(bf16[4,128,128]{2,1,0:T(8,128)(2,1)} %param.15), channel_id=1, source_target_pairs={{0,2},{1,3},{2,0},{3,1},{4,6},{5,7},{6,4},{7,5},{8,10},{9,11},{10,... | collective-permute-start | bytes 393224 | tf_op jit(solution)/shard_map/ppermute | solution.py:152
  3.8 10.2 %collective-permute-start.10 = (bf16[4,32,128]{2,1,0:T(8,128)(2,1)S(1)}, bf16[4,32,128]{2,1,0:T(8,128)(2,1)S(1)}, u32[]{:S(2)}, u32[]{:S(2)}) collective-permute-start(bf16[4,32,128]{2,1,0:T(8,128)(2,1)S(1)} %get-tuple-element.26), channel_id=1, source_target_pairs={{0,8},{1,9},{2,10},{3,11},{4,12},{5,13},{6,14},{7,15},{8,0},{9,1},... | collective-permute-start | bytes 98312 | tf_op jit(solution)/shard_map/ppermute | solution.py:152
  5.5 8.6 %collective-permute-start.11 = (bf16[4,32,128]{2,1,0:T(8,128)(2,1)S(1)}, bf16[4,32,128]{2,1,0:T(8,128)(2,1)S(1)}, u32[]{:S(2)}, u32[]{:S(2)}) collective-permute-start(bf16[4,32,128]{2,1,0:T(8,128)(2,1)S(1)} %get-tuple-element.28), channel_id=1, source_target_pairs={{0,16},{1,17},{2,18},{3,19},{4,20},{5,21},{6,22},{7,23},{8,24},{9,... | collective-permute-start | bytes 98312 | tf_op jit(solution)/shard_map/ppermute | solution.py:152
  8.1 7.6 %collective-permute-start.12 = (bf16[4,32,128]{2,1,0:T(8,128)(2,1)S(1)}, bf16[4,32,128]{2,1,0:T(8,128)(2,1)S(1)}, u32[]{:S(2)}, u32[]{:S(2)}) collective-permute-start(bf16[4,32,128]{2,1,0:T(8,128)(2,1)S(1)} %get-tuple-element.27), channel_id=1, source_target_pairs={{0,24},{1,25},{2,26},{3,27},{4,28},{5,29},{6,30},{7,31},{8,16},{9,... | collective-permute-start | bytes 98312 | tf_op jit(solution)/shard_map/ppermute | solution.py:152
  13.4 10.8 %copy-start.17 = (pred[8]{0:T(512)(128)(4,1)}, pred[8]{0:T(512)(128)(4,1)S(1)}, u32[]{:S(2)}) copy-start(pred[8]{0:T(512)(128)(4,1)S(1)} %compare_and_fusion) | copy-start | bytes 28
  14.1 5.8 %collective-permute-start.5 = (bf16[4,128,128]{2,1,0:T(8,128)(2,1)}, bf16[4,128,128]{2,1,0:T(8,128)(2,1)S(1)}, u32[]{:S(2)}, u32[]{:S(2)}) collective-permute-start(bf16[4,128,128]{2,1,0:T(8,128)(2,1)} %param.15), channel_id=1, source_target_pairs={{0,3},{1,2},{2,1},{3,0},{4,7},{5,6},{6,5},{7,4},{8,11},{9,10},{10,... | collective-permute-start | bytes 393224 | tf_op jit(solution)/shard_map/ppermute | solution.py:152
  14.1 6.6 %collective-permute-start.6 = (bf16[4,128,128]{2,1,0:T(8,128)(2,1)}, bf16[4,128,128]{2,1,0:T(8,128)(2,1)S(1)}, u32[]{:S(2)}, u32[]{:S(2)}) collective-permute-start(bf16[4,128,128]{2,1,0:T(8,128)(2,1)} %param.15), channel_id=1, source_target_pairs={{0,4},{1,5},{2,6},{3,7},{4,0},{5,1},{6,2},{7,3},{8,12},{9,13},{10,... | collective-permute-start | bytes 393224 | tf_op jit(solution)/shard_map/ppermute | solution.py:152
  15.7 12.5 %collective-permute-start.7 = (bf16[4,128,128]{2,1,0:T(8,128)(2,1)S(1)}, bf16[4,128,128]{2,1,0:T(8,128)(2,1)S(1)}, u32[]{:S(2)}, u32[]{:S(2)}) collective-permute-start(bf16[4,128,128]{2,1,0:T(8,128)(2,1)S(1)} %copy-done.1), channel_id=1, source_target_pairs={{0,5},{1,4},{2,7},{3,6},{4,1},{5,0},{6,3},{7,2},{8,13},{9,12},{10,... | collective-permute-start | bytes 393224 | tf_op jit(solution)/shard_map/ppermute | solution.py:152
  17.0 15.2 %collective-permute-start.8 = (bf16[4,128,128]{2,1,0:T(8,128)(2,1)S(1)}, bf16[4,128,128]{2,1,0:T(8,128)(2,1)S(1)}, u32[]{:S(2)}, u32[]{:S(2)}) collective-permute-start(bf16[4,128,128]{2,1,0:T(8,128)(2,1)S(1)} %copy-done.1), channel_id=1, source_target_pairs={{0,6},{1,7},{2,4},{3,5},{4,2},{5,3},{6,0},{7,1},{8,14},{9,15},{10,... | collective-permute-start | bytes 393224 | tf_op jit(solution)/shard_map/ppermute | solution.py:152
  19.7 12.5 %collective-permute-start.9 = (bf16[4,128,128]{2,1,0:T(8,128)(2,1)S(1)}, bf16[4,128,128]{2,1,0:T(8,128)(2,1)S(1)}, u32[]{:S(2)}, u32[]{:S(2)}) collective-permute-start(bf16[4,128,128]{2,1,0:T(8,128)(2,1)S(1)} %copy-done.1), channel_id=1, source_target_pairs={{0,7},{1,6},{2,5},{3,4},{4,3},{5,2},{6,1},{7,0},{8,15},{9,14},{10,... | collective-permute-start | bytes 393224 | tf_op jit(solution)/shard_map/ppermute | solution.py:152
  19.8 14.1 %collective-permute-start = (bf16[4,128,128]{2,1,0:T(8,128)(2,1)S(1)}, bf16[4,128,128]{2,1,0:T(8,128)(2,1)S(1)}, u32[]{:S(2)}, u32[]{:S(2)}) collective-permute-start(bf16[4,128,128]{2,1,0:T(8,128)(2,1)S(1)} %copy-done.1), channel_id=1, source_target_pairs={{0,8},{1,9},{2,10},{3,11},{4,12},{5,13},{6,14},{7,15},{8,0},{9,1},... | collective-permute-start | bytes 393224 | tf_op jit(solution)/shard_map/ppermute | solution.py:152
  20.7 13.2 %collective-permute-start.1 = (bf16[4,128,128]{2,1,0:T(8,128)(2,1)S(1)}, bf16[4,128,128]{2,1,0:T(8,128)(2,1)S(1)}, u32[]{:S(2)}, u32[]{:S(2)}) collective-permute-start(bf16[4,128,128]{2,1,0:T(8,128)(2,1)S(1)} %copy-done.1), channel_id=1, source_target_pairs={{0,16},{1,17},{2,18},{3,19},{4,20},{5,21},{6,22},{7,23},{8,24},{9,... | collective-permute-start | bytes 393224 | tf_op jit(solution)/shard_map/ppermute | solution.py:152
  24.2 13.0 %copy-start.14 = (f32[128]{0:T(128)S(1)}, f32[128]{0:T(128)}, u32[]{:S(2)}) copy-start(f32[128]{0:T(128)} %param.18) | copy-start | bytes 1540
  24.2 13.0 %copy-start.18 = (f32[128]{0:T(128)S(1)}, f32[128]{0:T(128)}, u32[]{:S(2)}) copy-start(f32[128]{0:T(128)} %param.19) | copy-start | bytes 1540
  28.2 8.2 %collective-permute-start.2 = (bf16[4,128,128]{2,1,0:T(8,128)(2,1)S(1)}, bf16[4,128,128]{2,1,0:T(8,128)(2,1)S(1)}, u32[]{:S(2)}, u32[]{:S(2)}) collective-permute-start(bf16[4,128,128]{2,1,0:T(8,128)(2,1)S(1)} %copy-done.1), channel_id=1, source_target_pairs={{0,24},{1,25},{2,26},{3,27},{4,28},{5,29},{6,30},{7,31},{8,16},{9,... | collective-permute-start | bytes 393224 | tf_op jit(solution)/shard_map/ppermute | solution.py:152
  32.2 5.8 %copy-start.10 = (bf16[128,128]{1,0:T(8,128)(2,1)S(1)}, bf16[128,128]{1,0:T(8,128)(2,1)}, u32[]{:S(2)}) copy-start(bf16[128,128]{1,0:T(8,128)(2,1)} %param.21) | copy-start | bytes 98308
  38.0 0.8 copy-start.19
  38.8 4.1 %copy-start.6 = (f32[128,16,128]{2,0,1:T(8,128)}, f32[128,16,128]{2,0,1:T(8,128)S(1)}, u32[]{:S(2)}) copy-start(f32[128,16,128]{2,0,1:T(8,128)S(1)} %fusion.20) | copy-start | bytes 3145732
  38.8 1.4 %copy-start.11 = (bf16[128,128]{1,0:T(8,128)(2,1)S(1)}, bf16[128,128]{1,0:T(8,128)(2,1)}, u32[]{:S(2)}) copy-start(bf16[128,128]{1,0:T(8,128)(2,1)} %param.22) | copy-start | bytes 98308
  40.2 2.7 %copy-start.2 = (f32[32,128,128]{1,2,0:T(8,128)}, f32[32,128,128]{1,2,0:T(8,128)S(1)}, u32[]{:S(2)}) copy-start(f32[32,128,128]{1,2,0:T(8,128)S(1)} %add_divide_fusion) | copy-start | bytes 6291460
  40.2 2.7 %copy-start.9 = (bf16[128,128]{1,0:T(8,128)(2,1)S(1)}, bf16[128,128]{1,0:T(8,128)(2,1)}, u32[]{:S(2)}) copy-start(bf16[128,128]{1,0:T(8,128)(2,1)} %param.20) | copy-start | bytes 98308
  44.3 2.7 %copy-start.13 = (bf16[128,128]{1,0:T(8,128)(2,1)S(1)}, bf16[128,128]{1,0:T(8,128)(2,1)}, u32[]{:S(2)}) copy-start(bf16[128,128]{1,0:T(8,128)(2,1)} %param.24) | copy-start | bytes 98308
  44.3 2.7 %copy-start.21 = (pred[32]{0:T(512)(128)(4,1)S(1)}, pred[32]{0:T(512)(128)(4,1)}, u32[]{:S(2)}) copy-start(pred[32]{0:T(512)(128)(4,1)} %broadcast_in_dim.18) | copy-start | bytes 100
  44.3 3.0 %copy-start.16 = (f32[128]{0:T(128)S(1)}, f32[128]{0:T(128)}, u32[]{:S(2)}) copy-start(f32[128]{0:T(128)} %param.25) | copy-start | bytes 1540
  52.2 2.9 %copy-start.7 = (f32[128,16,128]{2,0,1:T(8,128)S(1)}, f32[128,16,128]{2,0,1:T(8,128)}, u32[]{:S(2)}) copy-start(f32[128,16,128]{2,0,1:T(8,128)} %copy-done.6) | copy-start | bytes 3145732
  52.2 3.0 %copy-start.8 = (f32[128,16,128]{2,0,1:T(8,128)S(1)}, f32[128,16,128]{2,0,1:T(8,128)}, u32[]{:S(2)}) copy-start(f32[128,16,128]{2,0,1:T(8,128)} %get-tuple-element.32) | copy-start | bytes 3145732
  55.1 7.0 %copy-start.5 = (f32[128,32,128]{2,1,0:T(8,128)S(1)}, f32[128,32,128]{2,1,0:T(8,128)}, u32[]{:S(2)}) copy-start(f32[128,32,128]{2,1,0:T(8,128)} %fusion.48) | copy-start | bytes 6291460
  57.0 5.2 %copy-start.4 = (f32[32,128,128]{1,2,0:T(8,128)S(1)}, f32[32,128,128]{1,2,0:T(8,128)}, u32[]{:S(2)}) copy-start(f32[32,128,128]{1,2,0:T(8,128)} %get-tuple-element.30) | copy-start | bytes 6291460
  57.5 4.7 %copy-start.3 = (f32[32,128,128]{1,2,0:T(8,128)S(1)}, f32[32,128,128]{1,2,0:T(8,128)}, u32[]{:S(2)}) copy-start(f32[32,128,128]{1,2,0:T(8,128)} %copy-done.2) | copy-start | bytes 6291460
  57.7 8.5 %collective-permute-start.13 = (bf16[4,128,128]{2,1,0:T(8,128)(2,1)S(1)}, bf16[4,128,128]{2,1,0:T(8,128)(2,1)S(1)}, u32[]{:S(2)}, u32[]{:S(2)}) collective-permute-start(bf16[4,128,128]{2,1,0:T(8,128)(2,1)S(1)} %get-tuple-element.22), channel_id=1, source_target_pairs={{0,8},{1,9},{2,10},{3,11},{4,12},{5,13},{6,14},{7,15},{8,0},{9,1},... | collective-permute-start | bytes 393224 | tf_op jit(solution)/shard_map/ppermute | solution.py:152
  59.3 12.7 %collective-permute-start.14 = (bf16[4,128,128]{2,1,0:T(8,128)(2,1)S(1)}, bf16[4,128,128]{2,1,0:T(8,128)(2,1)S(1)}, u32[]{:S(2)}, u32[]{:S(2)}) collective-permute-start(bf16[4,128,128]{2,1,0:T(8,128)(2,1)S(1)} %get-tuple-element.24), channel_id=1, source_target_pairs={{0,16},{1,17},{2,18},{3,19},{4,20},{5,21},{6,22},{7,23},{8,24},{9,... | collective-permute-start | bytes 393224 | tf_op jit(solution)/shard_map/ppermute | solution.py:152
  61.8 11.8 %collective-permute-start.15 = (bf16[4,128,128]{2,1,0:T(8,128)(2,1)S(1)}, bf16[4,128,128]{2,1,0:T(8,128)(2,1)S(1)}, u32[]{:S(2)}, u32[]{:S(2)}) collective-permute-start(bf16[4,128,128]{2,1,0:T(8,128)(2,1)S(1)} %get-tuple-element.23), channel_id=1, source_target_pairs={{0,24},{1,25},{2,26},{3,27},{4,28},{5,29},{6,30},{7,31},{8,16},{9,... | collective-permute-start | bytes 393224 | tf_op jit(solution)/shard_map/ppermute | solution.py:152
  62.2 1.6 %copy-start.12 = (bf16[128,128]{1,0:T(8,128)(2,1)S(1)}, bf16[128,128]{1,0:T(8,128)(2,1)}, u32[]{:S(2)}) copy-start(bf16[128,128]{1,0:T(8,128)(2,1)} %param.22) | copy-start | bytes 98308
  62.2 1.6 %copy-start.20 = (bf16[128,128]{1,0:T(8,128)(2,1)S(1)}, bf16[128,128]{1,0:T(8,128)(2,1)}, u32[]{:S(2)}) copy-start(bf16[128,128]{1,0:T(8,128)(2,1)} %param.23) | copy-start | bytes 98308
  63.8 21.2 %copy-start.15 = (f32[128]{0:T(128)S(1)}, f32[128]{0:T(128)}, u32[]{:S(2)}) copy-start(f32[128]{0:T(128)} %param.18) | copy-start | bytes 1540
  64.7 8.9 %collective-permute-start.16 = (bf16[4,128,128]{2,1,0:T(8,128)(2,1)S(1)}, bf16[4,128,128]{2,1,0:T(8,128)(2,1)S(1)}, u32[]{:S(2)}, u32[]{:S(2)}) collective-permute-start(bf16[4,128,128]{2,1,0:T(8,128)(2,1)S(1)} %get-tuple-element.15), channel_id=1, source_target_pairs={{0,1},{1,0},{2,3},{3,2},{4,5},{5,4},{6,7},{7,6},{8,9},{9,8},{10,11... | collective-permute-start | bytes 393224 | tf_op jit(solution)/shard_map/ppermute | solution.py:152
  64.7 9.1 %collective-permute-start.17 = (bf16[4,128,128]{2,1,0:T(8,128)(2,1)S(1)}, bf16[4,128,128]{2,1,0:T(8,128)(2,1)S(1)}, u32[]{:S(2)}, u32[]{:S(2)}) collective-permute-start(bf16[4,128,128]{2,1,0:T(8,128)(2,1)S(1)} %get-tuple-element.21), channel_id=1, source_target_pairs={{0,2},{1,3},{2,0},{3,1},{4,6},{5,7},{6,4},{7,5},{8,10},{9,11},{10,... | collective-permute-start | bytes 393224 | tf_op jit(solution)/shard_map/ppermute | solution.py:152
  66.2 10.3 %collective-permute-start.18 = (bf16[4,128,128]{2,1,0:T(8,128)(2,1)S(1)}, bf16[4,128,128]{2,1,0:T(8,128)(2,1)S(1)}, u32[]{:S(2)}, u32[]{:S(2)}) collective-permute-start(bf16[4,128,128]{2,1,0:T(8,128)(2,1)S(1)} %get-tuple-element.20), channel_id=1, source_target_pairs={{0,3},{1,2},{2,1},{3,0},{4,7},{5,6},{6,5},{7,4},{8,11},{9,10},{10,... | collective-permute-start | bytes 393224 | tf_op jit(solution)/shard_map/ppermute | solution.py:152
  72.0 11.0 %collective-permute-start.19 = (bf16[4,128,128]{2,1,0:T(8,128)(2,1)S(1)}, bf16[4,128,128]{2,1,0:T(8,128)(2,1)S(1)}, u32[]{:S(2)}, u32[]{:S(2)}) collective-permute-start(bf16[4,128,128]{2,1,0:T(8,128)(2,1)S(1)} %get-tuple-element.19), channel_id=1, source_target_pairs={{0,4},{1,5},{2,6},{3,7},{4,0},{5,1},{6,2},{7,3},{8,12},{9,13},{10,... | collective-permute-start | bytes 393224 | tf_op jit(solution)/shard_map/ppermute | solution.py:152
  73.6 11.4 %collective-permute-start.20 = (bf16[4,128,128]{2,1,0:T(8,128)(2,1)S(1)}, bf16[4,128,128]{2,1,0:T(8,128)(2,1)S(1)}, u32[]{:S(2)}, u32[]{:S(2)}) collective-permute-start(bf16[4,128,128]{2,1,0:T(8,128)(2,1)S(1)} %get-tuple-element.18), channel_id=1, source_target_pairs={{0,5},{1,4},{2,7},{3,6},{4,1},{5,0},{6,3},{7,2},{8,13},{9,12},{10,... | collective-permute-start | bytes 393224 | tf_op jit(solution)/shard_map/ppermute | solution.py:152
  73.6 11.4 %collective-permute-start.21 = (bf16[4,128,128]{2,1,0:T(8,128)(2,1)S(1)}, bf16[4,128,128]{2,1,0:T(8,128)(2,1)S(1)}, u32[]{:S(2)}, u32[]{:S(2)}) collective-permute-start(bf16[4,128,128]{2,1,0:T(8,128)(2,1)S(1)} %get-tuple-element.17), channel_id=1, source_target_pairs={{0,6},{1,7},{2,4},{3,5},{4,2},{5,3},{6,0},{7,1},{8,14},{9,15},{10,... | collective-permute-start | bytes 393224 | tf_op jit(solution)/shard_map/ppermute | solution.py:152
  73.8 11.2 %collective-permute-start.22 = (bf16[4,128,128]{2,1,0:T(8,128)(2,1)S(1)}, bf16[4,128,128]{2,1,0:T(8,128)(2,1)S(1)}, u32[]{:S(2)}, u32[]{:S(2)}) collective-permute-start(bf16[4,128,128]{2,1,0:T(8,128)(2,1)S(1)} %get-tuple-element.16), channel_id=1, source_target_pairs={{0,7},{1,6},{2,5},{3,4},{4,3},{5,2},{6,1},{7,0},{8,15},{9,14},{10,... | collective-permute-start | bytes 393224 | tf_op jit(solution)/shard_map/ppermute | solution.py:152

commit v3 on v2

--- a/solution.py
+++ b/solution.py
@@ -147,22 +147,18 @@
     me = lax.axis_index("dap")
     place, level = me % plane, me // plane
     span = plane * own
-
-    def send(value, mask):
-        return lax.ppermute(value, "dap", [(i, i ^ mask) for i in range(dap)])
-
-    row_acts = [pair_act] + [send(pair_act, t * plane) for t in range(1, column)]
-    col_acts = [pair_act] + [send(pair_act, s) for s in range(1, plane)]
-    grads = []
-    for t in range(column):
-        part = lax.dynamic_slice_in_dim(out_grad, (level ^ t) * span, span, 1)
-        grads.append(send(part, t * plane) if t else part)
-    upstream = jnp.concatenate(grads, axis=0).astype(jnp.float32)
-    row_act = jnp.concatenate(row_acts, axis=0)
-    col_act = jnp.concatenate(col_acts, axis=0)
+    planes = [[p * plane + q for q in range(plane)] for p in range(column)]
+    columns = [[p * plane + q for p in range(column)] for q in range(plane)]
+    col_act = lax.all_gather(pair_act, "dap", axis_index_groups=planes, tiled=True)
+    row_act = lax.all_gather(pair_act, "dap", axis_index_groups=columns, tiled=True)
+    upstream = jnp.swapaxes(out_grad.reshape(own, column, span, chan), 0, 1)
+    upstream = lax.all_to_all(
+        upstream, "dap", split_axis=0, concat_axis=0, axis_index_groups=columns, tiled=True
+    )
+    upstream = upstream.reshape(column * own, span, chan).astype(jnp.float32)
     valid = residue_mask.astype(jnp.float32)
-    ids_row = jnp.concatenate([(me ^ (t * plane)) * own + jnp.arange(own) for t in range(column)])
-    ids_col = jnp.concatenate([(me ^ s) * own + jnp.arange(own) for s in range(plane)])
+    ids_row = jnp.concatenate([(p * plane + place) * own + jnp.arange(own) for p in range(column)])
+    ids_col = level * span + jnp.arange(span)
 
     def edges(act, ids, w_proj, w_sig):
         normed, _ = normalise(act.astype(jnp.float32), 2)
@@ -176,19 +172,12 @@
 
     norm_a, a_proj, a_sig, mask_a, edge_a = edges(row_act, ids_row, w_a_proj, w_a_gate)
     _, b_proj, b_sig, mask_b, edge_b = edges(col_act, ids_col, w_b_proj, w_b_gate)
-    order = jnp.bitwise_xor(place, jnp.arange(plane))
-
-    def to_slots(value):
-        value = value.reshape(value.shape[0], plane, own, chan)
-        return jnp.take(value, order, axis=1).reshape(-1, span, chan)
-
     tri = jnp.einsum("hik,hjk->hij", edge_a, edge_b, preferred_element_type=jnp.float32)
     normed_out, rstd_out = normalise(tri.astype(jnp.bfloat16).astype(jnp.float32), 0)
     gain_out = ln_out_gain.reshape(-1, 1, 1)
     tri_norm = (normed_out * gain_out + ln_out_bias.reshape(-1, 1, 1)).astype(jnp.bfloat16)
     proj_out = jnp.einsum("hij,hc->ijc", tri_norm, w_out, preferred_element_type=jnp.float32)
-    norm_tile = to_slots(lax.dynamic_slice_in_dim(norm_a, level * span, span, 1))
-    upstream = to_slots(upstream)
+    norm_tile = lax.dynamic_slice_in_dim(norm_a, level * span, span, 1)
     gate_act = jax.nn.sigmoid(
         jnp.einsum("ijc,cd->ijd", norm_tile, w_gate, preferred_element_type=jnp.float32)
     )
@@ -212,17 +201,17 @@
     share_b = back(d_edge_b, mask_b, b_sig, b_proj, w_b_proj, w_b_gate).astype(jnp.bfloat16)
     share_a = back(d_edge_a, mask_a, a_sig, a_proj, w_a_proj, w_a_gate)
     gate_part = jnp.einsum("ijd,cd->ijc", d_gate, w_gate, preferred_element_type=jnp.float32)
-    gate_part = to_slots(gate_part)
     old = lax.dynamic_slice_in_dim(share_a, level * span, span, 1)
     share_a = lax.dynamic_update_slice_in_dim(share_a, old + gate_part, level * span, 1)
     share_a = share_a.astype(jnp.bfloat16)
-    total = jnp.zeros(pair_act.shape, jnp.float32)
-    for t in range(column):
-        part = share_a[t * own : (t + 1) * own]
-        total = total + (send(part, t * plane) if t else part).astype(jnp.float32)
-    for s in range(plane):
-        part = share_b[s * own : (s + 1) * own]
-        total = total + (send(part, s) if s else part).astype(jnp.float32)
+    share_a = lax.all_to_all(
+        share_a, "dap", split_axis=0, concat_axis=0, axis_index_groups=columns, tiled=True
+    ).reshape(column, *pair_act.shape)
+    share_b = lax.all_to_all(
+        share_b, "dap", split_axis=0, concat_axis=0, axis_index_groups=planes, tiled=True
+    ).reshape(plane, *pair_act.shape)
+    total = jnp.sum(share_a.astype(jnp.float32), axis=0)
+    total = total + jnp.sum(share_b.astype(jnp.float32), axis=0)
     normed_in, rstd_in = normalise(pair_act.astype(jnp.float32), 2)
     return norm_backward(total * ln_in_gain, normed_in, rstd_in, 2).astype(jnp.bfloat16)
 

time: 86.7 us -> 106 us (1.22)
  blocking collectives: 0 us -> 16.8 us
  starting transfers between devices: 31.2 us -> 15 us
  between operations: 0.76 us -> 13.7 us
  matrix products: 13.9 us -> 17.7 us
  waiting for transfers between devices: 20.1 us -> 21.3 us
    ppermute x23 -> x0, starting transfers between devices: 31.2 us -> none  [send(): return lax.ppermute(value, 'dap', [(i, i ^ mask) for i in range(dap)])]
    all_to_all x0 -> x3, waiting for transfers between devices: none -> 20.5 us  [the longest x1 14.9 us: gather_tiles(): lax.all_to_all(share_b, 'dap', split_axis=0, concat_axis=0, axis_index_gr...]
    ppermute x23 -> x0, waiting for transfers between devices: 20.1 us -> none  [send(): return lax.ppermute(value, 'dap', [(i, i ^ mask) for i in range(dap)])]
    all_gather x0 -> x1, blocking collectives: none -> 16.8 us  [gather_tiles(): lax.all_gather(pair_act, 'dap', axis_index_groups=columns, tiled=True)]
    all_to_all x0 -> x3, starting transfers between devices: none -> 15 us  [the longest x1 6.45 us: gather_tiles(): lax.all_to_all(upstream, 'dap', split_axis=0, concat_axis=0, axis_index_g...]
    gather x3 -> x0, local copies, waits for them, and re-layouts: 1.83 us -> none  [to_slots(): return jnp.take(value, order, axis=1).reshape(-1, span, chan)]
    convert_element_type x1, local copies, waits for them, and re-layouts: 0.43 us -> 2.11 us  [gather_tiles(): norm_backward(d_normed, normed_out, rstd_out, 0).astype(jnp.bfloat16)]
    reshape x1, local copies, waits for them, and re-layouts: 0.16 us -> 1.57 us  [gather_tiles(): upstream = jnp.swapaxes(out_grad.reshape(own, column, span, chan), 0, 1)]
  transfers between devices with their start and end apart: 23 -> 4, of which waited for: 6 -> 2; matrix products, arithmetic and copies ran while one was open for 14% -> 25% of each run, Pallas kernels for 0% -> 0%
where the time goes in v3:
time: 106 us; the launch traced here: 105 us
  waiting for transfers between devices  21.3 us (20%)
  matrix products  17.7 us (17%)
  blocking collectives  16.8 us (16%)
  starting transfers between devices  15 us (14%)
  between operations  13.7 us (13%)
  other arithmetic  12.8 us (12%)
  local copies, waits for them, and re-layouts  7.7 us (7%)
    all_gather x1, blocking collectives, gather_tiles(): lax.all_gather(pair_act, 'dap', axis_index_groups=columns, tiled=True)  16.8 us
    all_to_all x1, waiting for transfers between devices, gather_tiles(): lax.all_to_all(share_b, 'dap', split_axis=0, concat_axis=0, axis_index_gr...  14.9 us
    all_to_all x1, starting transfers between devices, gather_tiles(): lax.all_to_all(upstream, 'dap', split_axis=0, concat_axis=0, axis_index_g...  6.45 us
    all_to_all x1, waiting for transfers between devices, gather_tiles(): lax.all_to_all(share_a, 'dap', split_axis=0, concat_axis=0, axis_index_gr...  5.61 us
    all_to_all x1, starting transfers between devices, gather_tiles(): lax.all_to_all(share_a, 'dap', split_axis=0, concat_axis=0, axis_index_gr...  4.83 us
    dot_general x2, matrix products, edges(): jnp.einsum('ikc,ch->hik', pair_norm, w_proj, preferred_element_type=jnp.f...  4.22 us
    all_to_all x1, starting transfers between devices, gather_tiles(): lax.all_to_all(share_b, 'dap', split_axis=0, concat_axis=0, axis_index_gr...  3.73 us
    reduce_sum x4, other arithmetic, normalise(): jnp.mean(centre * centre, axis=reduce_dim, keepdims=True) + EPSILON  3.46 us
  transfers between devices with their start and end apart: 4, of which 2 were waited for; matrix products, arithmetic and copies ran while one was open for 25% of the time, Pallas kernels for 0%

profile of v3, /device:TPU:0, one launch (start us, length us, event | category | flops | bytes accessed | tf_op | source)
XLA Modules:
  0.0 105.0 jit_solution(3630144720170163534)
XLA Ops:
  6.5 0.7 all-gather.2.cloned.1.call-update
  7.3 1.6 %copy.106 = bf16[4,4,32,128]{3,2,0,1:T(8,128)(2,1)} copy(bf16[4,4,32,128]{3,2,1,0:T(8,128)(2,1)} %bitcast.92) | data formatting | bytes 262144 | tf_op jit(solution)/shard_map/reshape | solution.py:154
  8.8 6.4 %all-to-all-start = ((bf16[4,4,32,128]{3,2,1,0:T(8,128)(2,1)}), bf16[4,4,32,128]{3,2,1,0:T(8,128)(2,1)S(1)}, u32[]{:S(2)}, u32[]{:S(2)}) async-start(bf16[4,4,32,128]{3,2,1,0:T(8,128)(2,1)} %bitcast.87), calls=%async_computation | async-start | bytes 262144 | tf_op jit(solution)/shard_map/all_to_all | solution.py:155
  15.3 16.8 %all_gather.6 = bf16[16,128,128]{2,1,0:T(8,128)(2,1)S(1)} all-gather(bf16[4,128,128]{2,1,0:T(8,128)(2,1)} %param.13), channel_id=1, replica_groups={{0,8,16,24},{1,9,17,25},{2,10,18,26},{3,11,19,27},{4,12,20,28},{5,13,21..., dimensions={0}, use_global_device_ids=true | all-gather | bytes 655360 | tf_op jit(solution)/shard_map/all_gather | solution.py:153
  32.1 0.7 convert_element_type.82
  32.8 0.1 fusion.102
  32.9 0.7 gather_fusion
  33.6 0.7 gather_fusion.1
  34.3 0.2 convert_reduce_fusion.2
  34.5 0.6 fusion.31
  35.1 0.1 broadcast_multiply_fusion.6
  35.2 0.1 broadcast_multiply_fusion.1
  35.3 0.6 fusion.34
  35.9 0.9 fusion.29
  36.9 0.5 fusion.20
  37.4 1.0 copy-done.5
  38.3 1.5 %multiply_convert_fusion.1 = (bf16[128,16,128]{2,0,1:T(8,128)(2,1)}, f32[128,16,128]{2,0,1:T(8,128)}) fusion(f32[128,16,128]{2,0,1:T(8,128)S(1)} %fusion.20, f32[16,128]{1,0:T(8,128)S(1)} %broadcast_multiply_fusion.6, bf16[16,128,128]{2,1,0:T(8,128)(2,1)S(1)} %fusion.34, bf16[128,128]{1,0:T(8,128)(2,1)S(1)} %copy-done.8), kind=kOutput, calls=%fused_computation.61 | convolution fusion | flops 67895296 | bytes 3186688 | tf_op jit(solution)/shard_map/ikc,ch->hik/dot_general | solution.py:166
  39.8 1.7 %convert_reduce_fusion = f32[32,128]{1,0:T(8,128)S(1)} fusion(bf16[32,128,128]{2,1,0:T(8,128)(2,1)} %all-gather.2.cloned.1.call-done), kind=kLoop, calls=%fused_computation.3 | loop fusion | flops 1044480 | bytes 1064960 | tf_op jit(solution)/shard_map/reduce_sum | solution.py:10
  41.5 2.3 %fusion.2 = f32[32,128]{1,0:T(8,128)S(1)} fusion(bf16[32,128,128]{2,1,0:T(8,128)(2,1)} %all-gather.2.cloned.1.call-done, f32[32,128]{1,0:T(8,128)S(1)} %broadcast_multiply_fusion), kind=kLoop, calls=%fused_computation.6 | loop fusion | flops 2093056 | bytes 1081344 | tf_op jit(solution)/shard_map/reduce_sum | solution.py:11
  43.9 0.0 copy-start.10
  43.9 1.4 %add_divide_fusion = f32[32,128,128]{1,2,0:T(8,128)S(1)} fusion(bf16[32,128,128]{2,1,0:T(8,128)(2,1)S(1)} %copy-done.1, f32[128]{0:T(128)S(1)} %copy-done.15, f32[128]{0:T(128)S(1)} %copy-done.13, f32[32,128]{1,0:T(8,128)S(1)} %add_rsqrt_fusion, f32[32,128]{1,0:T(8,128)S(1)} %broadcast_multiply_fusion, bf16[128,128]{1,0:T(8,128)(2,1)S(1)} %copy-done.17), kind=kOutput, calls=%fused_computation.24 | convolution fusion | flops 138936320 | bytes 3212288 | tf_op jit(solution)/shard_map/ikc,ch->hik/dot_general | solution.py:168
  45.4 2.7 %fusion.10 = (bf16[128,32,128]{2,0,1:T(8,128)(2,1)S(1)}, f32[32,128,128]{1,2,0:T(8,128)}) fusion(f32[32,128,128]{1,2,0:T(8,128)S(1)} %add_divide_fusion, f32[32,128]{1,0:T(8,128)S(1)} %broadcast_multiply_fusion.1, bf16[128,128]{1,0:T(8,128)(2,1)S(1)} %copy-done.10, bf16[32,128,128]{2,1,0:T(8,128)(2,1)S(1)} %copy-done.1, f32[128]{0:T(128)S(1)} %copy-done.15, ...), kind=kOutput, calls=%fused_computation.17 | convolution fusion | flops 138936320 | bytes 6374400 | tf_op jit(solution)/shard_map/ikc,ch->hik/dot_general | solution.py:166
  48.1 1.9 %fusion.42 = bf16[128,16,32]{2,1,0:T(8,128)(2,1)} fusion(bf16[128,32,128]{2,0,1:T(8,128)(2,1)S(1)} %get-tuple-element.14, bf16[128,16,128]{2,0,1:T(8,128)(2,1)S(1)} %copy-done.4), kind=kOutput, calls=%fused_computation.64 | convolution fusion | flops 16777216 | bytes 1703936 | tf_op jit(solution)/shard_map/hik,hjk->hij/dot_general | solution.py:175
  50.0 1.4 %copy.63 = bf16[128,16,32]{0,2,1:T(8,128)(2,1)S(1)} copy(bf16[128,16,32]{2,1,0:T(8,128)(2,1)} %fusion.42) | data formatting | bytes 262144 | tf_op jit(solution)/shard_map/hik,hjk->hij/dot_general | solution.py:175
  51.4 0.1 convert_reduce_fusion.4
  51.6 0.3 fusion.71
  51.9 1.3 %fusion.108 = (f32[16,32]{1,0:T(8,128)S(1)}, f32[16,32]{1,0:T(8,128)S(1)}, f32[128,16,32]{0,2,1:T(8,128)S(1)}) fusion(f32[16,32]{1,0:T(8,128)S(1)} %add_rsqrt_fusion.1, f32[16,32]{1,0:T(8,128)S(1)} %broadcast_multiply_fusion.4, bf16[128,16,32]{0,2,1:T(8,128)(2,1)S(1)} %copy.63, f32[128]{0:T(128)S(1)} %copy-done.14, bf16[128,128]{1,0:T(8,128)(2,1)S(1)} %copy-done, ...), kind=kOutput, calls=%fused_computation.151 | convolution fusion | flops 17431552 | bytes 827904 | tf_op jit(solution)/shard_map/ijc,hc->hij/dot_general | solution.py:187
  53.2 1.0 fusion.68
  54.2 2.1 %copy.65 = bf16[128,16,32]{2,1,0:T(8,128)(2,1)} copy(bf16[128,16,32]{0,2,1:T(8,128)(2,1)} %fusion.68) | data formatting | bytes 262144 | tf_op jit(solution)/shard_map/convert_element_type | solution.py:189
  56.4 1.9 %fusion.40 = f32[128,16,128]{2,1,0:T(8,128)S(1)} fusion(bf16[128,16,32]{2,1,0:T(8,128)(2,1)} %copy.65, bf16[128,32,128]{2,0,1:T(8,128)(2,1)S(1)} %get-tuple-element.14), kind=kOutput, calls=%fused_computation.62 | convolution fusion | flops 16777216 | bytes 2228224 | tf_op jit(solution)/shard_map/hij,hjk->hik/dot_general | solution.py:190
  58.3 0.5 fusion.47
  58.8 0.5 fusion.35
  59.3 0.2 copy-done.16
  59.5 1.4 %fusion.23 = f32[16,128,128]{2,1,0:T(8,128)S(1)} fusion(f32[16,128,128]{2,1,0:T(8,128)S(1)} %fusion.35, s32[]{:T(128)S(6)} %select_n.40, f32[16,32,128]{2,1,0:T(8,128)} %fusion.29, bf16[16,32,128]{2,1,0:T(8,128)(2,1)S(1)} %bitcast.91, bf16[128,16,32]{0,2,1:T(8,128)(2,1)S(1)} %copy.63, f32[128]{0:T(128)S(1)} %copy-done.16, f32[128]{0:T(128)S(1)} %copy-done.14, ...), kind=kOutput, calls=%fused_computation.38 | convolution fusion | flops 34406400 | bytes 1131524 | tf_op jit(solution)/shard_map/ijd,cd->ijc/dot_general | solution.py:203
  60.8 0.9 convert_element_type.99
  61.7 4.8 %all-to-all-start.1 = ((bf16[16,128,128]{2,1,0:T(8,128)(2,1)}), bf16[16,128,128]{2,1,0:T(8,128)(2,1)S(1)}, u32[]{:S(2)}, u32[]{:S(2)}) async-start(bf16[16,128,128]{2,1,0:T(8,128)(2,1)} %convert_element_type.99), calls=%async_computation.1 | async-start | bytes 1048576 | tf_op jit(solution)/shard_map/all_to_all | solution.py:207
  66.6 1.9 %fusion.48 = f32[128,32,128]{2,1,0:T(8,128)S(1)} fusion(bf16[128,16,32]{2,1,0:T(8,128)(2,1)} %copy.65, bf16[128,16,128]{2,0,1:T(8,128)(2,1)} %get-tuple-element.16), kind=kOutput, calls=%fused_computation.68 | convolution fusion | flops 16777216 | bytes 2752512 | tf_op jit(solution)/shard_map/hij,hik->hjk/dot_general | solution.py:191
  68.5 1.6 %fusion.13 = (bf16[128,32,128]{2,0,1:T(8,128)(2,1)S(1)}, bf16[128,32,128]{2,0,1:T(8,128)(2,1)S(1)}) fusion(f32[32,128,128]{1,2,0:T(8,128)S(1)} %add_divide_fusion, f32[128,32,128]{2,1,0:T(8,128)S(1)} %fusion.48, f32[32,128]{1,0:T(8,128)S(1)} %broadcast_multiply_fusion.1, f32[32,128,128]{1,2,0:T(8,128)S(1)} %copy-done.2), kind=kLoop, calls=%fused_computation.25 | loop fusion | flops 3670016 | bytes 8404992 | tf_op jit(solution)/shard_map/convert_element_type | solution.py:195
  70.1 1.8 %fusion.14 = bf16[32,128,128]{2,1,0:T(8,128)(2,1)} fusion(bf16[128,32,128]{2,0,1:T(8,128)(2,1)S(1)} %get-tuple-element.11, bf16[128,32,128]{2,0,1:T(8,128)(2,1)S(1)} %get-tuple-element.10, bf16[128,128]{1,0:T(8,128)(2,1)S(1)} %copy-done.18, bf16[128,128]{1,0:T(8,128)(2,1)S(1)} %copy-done.11), kind=kOutput, calls=%fused_computation.26 | convolution fusion | flops 273285120 | bytes 3211264 | tf_op jit(solution)/shard_map/gik,cg->ikc/dot_general | solution.py:199
  71.9 5.6 %all-to-all-done.1 = bf16[16,128,128]{2,1,0:T(8,128)(2,1)S(1)} async-done(((bf16[16,128,128]{2,1,0:T(8,128)(2,1)}), bf16[16,128,128]{2,1,0:T(8,128)(2,1)S(1)}, u32[]{:S(2)}, u32[]{:S(2)}) %all-to-all-start.1) | async-done | bytes 524320 | tf_op jit(solution)/shard_map/all_to_all | solution.py:207
  77.5 3.7 %all-to-all-start.2 = ((bf16[32,128,128]{2,1,0:T(8,128)(2,1)}), bf16[32,128,128]{2,1,0:T(8,128)(2,1)S(1)}, u32[]{:S(2)}, u32[]{:S(2)}) async-start(bf16[32,128,128]{2,1,0:T(8,128)(2,1)} %fusion.14), calls=%async_computation.2 | async-start | bytes 2097152 | tf_op jit(solution)/shard_map/all_to_all | solution.py:210
  81.2 0.1 convert_reduce_fusion.5
  81.3 0.2 fusion.72
  81.6 0.1 convert_reduce_fusion.3
  81.7 14.9 %all-to-all-done.2 = bf16[32,128,128]{2,1,0:T(8,128)(2,1)S(1)} async-done(((bf16[32,128,128]{2,1,0:T(8,128)(2,1)}), bf16[32,128,128]{2,1,0:T(8,128)(2,1)S(1)}, u32[]{:S(2)}, u32[]{:S(2)}) %all-to-all-start.2) | async-done | bytes 1048608 | tf_op jit(solution)/shard_map/all_to_all | solution.py:210
  96.6 0.1 convert_reduce_fusion.1
  96.8 0.4 fusion.107
  97.2 1.0 fusion.64
  (55 shorter events, 0.2 us)
Async XLA Ops:
  6.5 45.3 %copy-start = (bf16[128,128]{1,0:T(8,128)(2,1)S(1)}, bf16[128,128]{1,0:T(8,128)(2,1)}, u32[]{:S(2)}) copy-start(bf16[128,128]{1,0:T(8,128)(2,1)} %param.25) | copy-start | bytes 98308
  6.5 28.7 %copy-start.13 = (f32[128]{0:T(128)S(1)}, f32[128]{0:T(128)}, u32[]{:S(2)}) copy-start(f32[128]{0:T(128)} %param.16) | copy-start | bytes 1540
  6.5 28.7 %copy-start.15 = (f32[128]{0:T(128)S(1)}, f32[128]{0:T(128)}, u32[]{:S(2)}) copy-start(f32[128]{0:T(128)} %param.17) | copy-start | bytes 1540
  6.5 33.3 %all-gather.2.cloned.1.call-start = ((), (), s32[]{:S(2)}) async-start(), calls=%async_computation.3 | async-start | bytes 1179648 | tf_op jit(solution)/shard_map/all_gather | solution.py:152
  8.8 27.1 %copy-start.12 = (bf16[128,128]{1,0:T(8,128)(2,1)S(1)}, bf16[128,128]{1,0:T(8,128)(2,1)}, u32[]{:S(2)}) copy-start(bf16[128,128]{1,0:T(8,128)(2,1)} %param.22) | copy-start | bytes 98308
  8.8 43.0 %all-to-all-start = ((bf16[4,4,32,128]{3,2,1,0:T(8,128)(2,1)}), bf16[4,4,32,128]{3,2,1,0:T(8,128)(2,1)S(1)}, u32[]{:S(2)}, u32[]{:S(2)}) async-start(bf16[4,4,32,128]{3,2,1,0:T(8,128)(2,1)} %bitcast.87), calls=%async_computation | async-start | bytes 262144 | tf_op jit(solution)/shard_map/all_to_all | solution.py:155
  32.9 4.0 %copy-start.9 = (bf16[128,128]{1,0:T(8,128)(2,1)S(1)}, bf16[128,128]{1,0:T(8,128)(2,1)}, u32[]{:S(2)}) copy-start(bf16[128,128]{1,0:T(8,128)(2,1)} %param.19) | copy-start | bytes 98308
  36.9 1.5 %copy-start.8 = (bf16[128,128]{1,0:T(8,128)(2,1)S(1)}, bf16[128,128]{1,0:T(8,128)(2,1)}, u32[]{:S(2)}) copy-start(bf16[128,128]{1,0:T(8,128)(2,1)} %param.18) | copy-start | bytes 98308
  37.4 1.0 copy-start.5
  38.3 5.5 %copy-start.17 = (bf16[128,128]{1,0:T(8,128)(2,1)S(1)}, bf16[128,128]{1,0:T(8,128)(2,1)}, u32[]{:S(2)}) copy-start(bf16[128,128]{1,0:T(8,128)(2,1)} %param.21) | copy-start | bytes 98308
  39.8 4.0 %copy-start.1 = (bf16[32,128,128]{2,1,0:T(8,128)(2,1)S(1)}, bf16[32,128,128]{2,1,0:T(8,128)(2,1)}, u32[]{:S(2)}) copy-start(bf16[32,128,128]{2,1,0:T(8,128)(2,1)} %all-gather.2.cloned.1.call-done) | copy-start | bytes 3145732
  43.9 1.4 %copy-start.10 = (bf16[128,128]{1,0:T(8,128)(2,1)S(1)}, bf16[128,128]{1,0:T(8,128)(2,1)}, u32[]{:S(2)}) copy-start(bf16[128,128]{1,0:T(8,128)(2,1)} %param.20) | copy-start | bytes 98308
  45.3 2.7 %copy-start.4 = (bf16[128,16,128]{2,0,1:T(8,128)(2,1)S(1)}, bf16[128,16,128]{2,0,1:T(8,128)(2,1)}, u32[]{:S(2)}) copy-start(bf16[128,16,128]{2,0,1:T(8,128)(2,1)} %get-tuple-element.16) | copy-start | bytes 1572868
  48.1 3.8 %copy-start.14 = (f32[128]{0:T(128)S(1)}, f32[128]{0:T(128)}, u32[]{:S(2)}) copy-start(f32[128]{0:T(128)} %param.23) | copy-start | bytes 1540
  56.3 1.9 %copy-start.6 = (f32[128,16,128]{2,0,1:T(8,128)S(1)}, f32[128,16,128]{2,0,1:T(8,128)}, u32[]{:S(2)}) copy-start(f32[128,16,128]{2,0,1:T(8,128)} %copy-done.5) | copy-start | bytes 3145732
  56.3 1.9 %copy-start.7 = (f32[128,16,128]{2,0,1:T(8,128)S(1)}, f32[128,16,128]{2,0,1:T(8,128)}, u32[]{:S(2)}) copy-start(f32[128,16,128]{2,0,1:T(8,128)} %get-tuple-element.17) | copy-start | bytes 3145732
  58.8 0.7 copy-start.16
  61.7 15.7 %all-to-all-start.1 = ((bf16[16,128,128]{2,1,0:T(8,128)(2,1)}), bf16[16,128,128]{2,1,0:T(8,128)(2,1)S(1)}, u32[]{:S(2)}, u32[]{:S(2)}) async-start(bf16[16,128,128]{2,1,0:T(8,128)(2,1)} %convert_element_type.99), calls=%async_computation.1 | async-start | bytes 1048576 | tf_op jit(solution)/shard_map/all_to_all | solution.py:207
  66.6 1.9 %copy-start.2 = (f32[32,128,128]{1,2,0:T(8,128)S(1)}, f32[32,128,128]{1,2,0:T(8,128)}, u32[]{:S(2)}) copy-start(f32[32,128,128]{1,2,0:T(8,128)} %get-tuple-element.15) | copy-start | bytes 6291460
  68.5 1.6 %copy-start.11 = (bf16[128,128]{1,0:T(8,128)(2,1)S(1)}, bf16[128,128]{1,0:T(8,128)(2,1)}, u32[]{:S(2)}) copy-start(bf16[128,128]{1,0:T(8,128)(2,1)} %param.20) | copy-start | bytes 98308
  68.5 1.6 %copy-start.18 = (bf16[128,128]{1,0:T(8,128)(2,1)S(1)}, bf16[128,128]{1,0:T(8,128)(2,1)}, u32[]{:S(2)}) copy-start(bf16[128,128]{1,0:T(8,128)(2,1)} %param.21) | copy-start | bytes 98308
  71.9 9.3 %copy-start.3 = (bf16[4,128,128]{2,1,0:T(8,128)(2,1)S(1)}, bf16[4,128,128]{2,1,0:T(8,128)(2,1)}, u32[]{:S(2)}) copy-start(bf16[4,128,128]{2,1,0:T(8,128)(2,1)} %param.13) | copy-start | bytes 393220
  77.5 19.1 %all-to-all-start.2 = ((bf16[32,128,128]{2,1,0:T(8,128)(2,1)}), bf16[32,128,128]{2,1,0:T(8,128)(2,1)S(1)}, u32[]{:S(2)}, u32[]{:S(2)}) async-start(bf16[32,128,128]{2,1,0:T(8,128)(2,1)} %fusion.14), calls=%async_computation.2 | async-start | bytes 2097152 | tf_op jit(solution)/shard_map/all_to_all | solution.py:210
Sparse Core Ops, SparseCore 0:
  9.3 26.1 all-gather.1
